TPU v7x, 32 devices: a whole 2x2x4 slice. The times are simulated.
32 devices in a mesh: lon: 8 (over y, x, core), lat: 4 (over z).
Axes of the slice: x: 2, y: 2, z: 4, core: 2. Of those that a mesh axis runs over, the one named last changes fastest.
Arguments:
- ocean_state: float32 [4, 8, 2048, 512], P(None, None, 'lon', 'lat'), may hold values from -6 to 6
- diffusivity: float32 [7, 2048, 512], P(None, 'lon', 'lat'), may hold values from 0.05 to 2
- land_mask: int32 [2048, 512], P('lon', 'lat'), may hold values from 0 to 1, as said below
- tile_plan: int32 [16, 4], P(None, 'lat'), may hold values from 0 to 15, as said below
Outputs:
- moved_state: float32 [4, 8, 2048, 512], P(None, None, 'lon', 'lat')
Inputs may be any that keep to these rules, and one draw needn't show every extreme that they name: `land_mask`: tiles of 128 x 128 columns may be land throughout; others are ocean throughout or mixed. Each column of tile_plan is a permutation of 0 to 15; a tile whose columns are all land keeps its position; every tile lands within 3 tile positions of where it stands, counted around the longitude loop; in some row one tile moves 3 positions east and one 3 positions west.
All inputs are finite; a program needn't handle non-finite values.
Results may differ from a plain program's by a relative error of at most 0.00002.
Values sent between devices are 32-bit elements; how exact they have to be, the bound alone decides.
A program may use at most 128 MiB of HBM per device.

v0:
```python
import jax
import jax.numpy as jnp
from jax import lax
from jax.sharding import PartitionSpec as P

advect_coef = 0.1
diffuse_coef = 0.1
gradient_coef = 0.1
thermal_coef = 0.2
haline_coef = 0.15
weight_coef = 0.25
mixing_coef = 1.0


def extended(cells, sides, width, closed):
    for axis, dim in sides:
        count = lax.axis_size(axis)
        ends = count if closed else count - 1
        head = lax.slice_in_dim(cells, 0, width, axis=dim)
        tail = lax.slice_in_dim(cells, cells.shape[dim] - width, cells.shape[dim], axis=dim)
        cells = jnp.concatenate(
            [
                lax.ppermute(tail, axis, [(i, (i + 1) % count) for i in range(ends)]),
                cells,
                lax.ppermute(head, axis, [((i + 1) % count, i) for i in range(ends)]),
            ],
            axis=dim,
        )
    return cells


def partner(value, axis, apart):
    mask = 2**apart
    pairs = [(source, source ^ mask) for source in range(lax.axis_size(axis))]
    return lax.ppermute(value, axis, pairs)


def from_behind(value, axis, by):
    length = lax.axis_size(axis)
    return lax.ppermute(value, axis, [(i, (i + by) % length) for i in range(length)])


def tendency(padded, wet_mask):
    center = padded[:, :, 1:-1, 1:-1]
    east_cells = padded[:, :, 2:, 1:-1]
    west_cells = padded[:, :, :-2, 1:-1]
    north_cells = padded[:, :, 1:-1, 2:]
    south_cells = padded[:, :, 1:-1, :-2]
    density = haline_coef * padded[1] - thermal_coef * padded[0]
    pressure = weight_coef * jnp.cumsum(density, axis=0)
    zonal_gradient = pressure[:, 2:, 1:-1] - pressure[:, :-2, 1:-1]
    merid_gradient = pressure[:, 1:-1, 2:] - pressure[:, 1:-1, :-2]
    zonal_flow = center[2]
    meridional = center[3]
    advect = -advect_coef * (
        zonal_flow * (east_cells - west_cells) + meridional * (north_cells - south_cells)
    )
    diffuse = diffuse_coef * (east_cells + west_cells + north_cells + south_cells - 4.0 * center)
    updated = center + advect + diffuse
    updated = updated.at[2].add(-gradient_coef * zonal_gradient)
    updated = updated.at[3].add(-gradient_coef * merid_gradient)
    return updated * wet_mask


def mix_columns(fields, diffusivity):
    levels = fields.shape[1]
    zero_band = jnp.zeros_like(diffusivity[0])
    lower_band = [zero_band] + [
        -mixing_coef * diffusivity[level_index - 1] for level_index in range(1, levels)
    ]
    upper_band = [-mixing_coef * diffusivity[level_index] for level_index in range(levels - 1)] + [
        zero_band
    ]
    sweep_upper = []
    sweep_rhs = []
    for level_index in range(levels):
        pivot_value = 1.0 - lower_band[level_index] - upper_band[level_index]
        rhs_level = fields[:, level_index]
        if level_index > 0:
            pivot_value = pivot_value - lower_band[level_index] * sweep_upper[level_index - 1]
            rhs_level = rhs_level - lower_band[level_index] * sweep_rhs[level_index - 1]
        sweep_upper.append(upper_band[level_index] / pivot_value)
        sweep_rhs.append(rhs_level / pivot_value)
    solution = [sweep_rhs[-1]]
    for level_index in range(levels - 2, -1, -1):
        solution.insert(0, sweep_rhs[level_index] - sweep_upper[level_index] * solution[0])
    return jnp.stack(solution, axis=1)


def nothing(fields, diffusivity):
    return jnp.zeros_like(fields)


def select_tile(candidates, offset, source_slot, tile_width):
    chosen = candidates[0][1]
    for candidate_offset, candidate_block in candidates[1:]:
        chosen = jnp.where(offset == candidate_offset, candidate_block, chosen)
    return jnp.where(source_slot == 0, chosen[:, :, :tile_width], chosen[:, :, tile_width:])


def local(ocean_state, diffusivity, land_mask, tile_plan):
    wet_mask = land_mask.astype(jnp.float32)
    fields = ocean_state * wet_mask
    lon_padded = extended(fields, (("lon", 2),), 1, True)
    padded = extended(lon_padded, (("lat", 3),), 1, False)
    fold_signs = jnp.array([1.0, 1.0, -1.0, -1.0], jnp.float32)[:, None, None]
    top_row = fields[:, :, :, -1]
    lon_count = lax.axis_size("lon")
    lon_position = lax.axis_index("lon")
    block_width = fields.shape[2]
    mirror = top_row
    for bit_index in range(lon_count.bit_length() - 1):
        mirror = partner(mirror, "lon", bit_index)
    mirror = mirror[:, :, ::-1]
    fold_ghost = mirror * fold_signs
    is_north = lax.axis_index("lat") == lax.axis_size("lat") - 1
    north_ghost = jnp.where(is_north, fold_ghost, padded[:, :, 1:-1, -1])
    padded = padded.at[:, :, 1:-1, -1].set(north_ghost)
    stepped = tendency(padded, wet_mask)
    tile_width = block_width // 2
    slot_results = []
    for slot_index in range(2):
        low_edge = slot_index * tile_width
        slot_fields = stepped[:, :, low_edge : low_edge + tile_width]
        slot_diffusivity = diffusivity[:, low_edge : low_edge + tile_width]
        slot_mask = wet_mask[low_edge : low_edge + tile_width]
        has_ocean = jnp.max(slot_mask) > 0.0
        slot_mixed = lax.cond(has_ocean, mix_columns, nothing, slot_fields, slot_diffusivity)
        slot_results.append(slot_mixed * slot_mask)
    tile_block = jnp.concatenate(slot_results, axis=2)
    from_west = from_behind(tile_block, "lon", 1)
    from_far_west = from_behind(tile_block, "lon", 2)
    from_east = from_behind(tile_block, "lon", -1)
    from_far_east = from_behind(tile_block, "lon", -2)
    candidates = [
        (0, tile_block),
        (-1, from_west),
        (-2, from_far_west),
        (1, from_east),
        (2, from_far_east),
    ]
    plan_row = tile_plan[:, 0]
    tile_total = plan_row.shape[0]
    positions = jnp.arange(tile_total, dtype=jnp.int32)
    new_tiles = []
    for slot_index in range(2):
        target = 2 * lon_position + slot_index
        source = jnp.sum(jnp.where(plan_row == target, positions, 0))
        offset = jnp.mod(source // 2 - lon_position + 2, lon_count) - 2
        new_tiles.append(select_tile(candidates, offset, source % 2, tile_width))
    return jnp.concatenate(new_tiles, axis=2)


def solution(mesh):
    placed = (P(None, None, "lon", "lat"), P(None, "lon", "lat"), P("lon", "lat"), P(None, "lat"))
    return jax.shard_map(
        local, mesh=mesh, in_specs=placed, out_specs=P(None, None, "lon", "lat"), check_vma=False
    )
```

profile of v0, /device:TPU:1, one launch (start us, length us, event | category | flops | bytes accessed | tf_op | source)
XLA Modules:
  0.0 409.1 jit_solution(16430421361281637154)
XLA Ops:
  1.0 5.4 %copy.28 = f32[4,8,256,128]{2,1,3,0:T(8,128)} copy(f32[4,8,256,128]{3,2,1,0:T(8,128)} %param.15) | data formatting | bytes 8388608 | tf_op args[0]
  6.5 2.6 broadcast_multiply_fusion.1
  16.0 2.6 collective-permute-start
  22.0 2.9 copy.33
  25.9 3.2 collective-permute-start.2
  35.3 7.1 %pad_maximum_fusion = f32[4,8,258,130]{2,1,0,3:T(8,128)} fusion(f32[4,8,258,1]{2,1,0,3:T(8,128)S(1)} %collective-permute-done.3, f32[4,8,1,128]{2,1,0,3:T(8,128)} %copy.33, f32[4,8,1,128]{2,1,0,3:T(8,128)S(1)} %copy.31, f32[4,8,258,1]{2,1,0,3:T(8,128)S(1)} %collective-permute-done.2, f32[4,8,256,128]{2,1,3,0:T(8,128)} %copy.28, f32[256,128]{0,1:T(8,128)S(1)} %copy.27), kind=kLoop, calls=%fused_computation.132 | loop fusion | flops 5341696 | bytes 8717312 | tf_op jit(solution)/shard_map/concatenate | solution.py:21
  44.6 3.5 fusion.63
  48.1 3.8 slice_bitcast_fusion.1
  51.9 9.5 %fusion.84 = (f32[4,8,256,128]{2,1,0,3:T(8,128)}, f32[4,8,256,128]{2,1,0,3:T(8,128)}, f32[4,8,256,128]{2,1,0,3:T(8,128)}, f32[4,8,256,128]{2,1,0,3:T(8,128)}, f32[4,8,256,128]{2,1,0,3:T(8,128)}) fusion(f32[4,8,258,130]{2,1,0,3:T(8,128)S(1)} %copy-done), kind=kLoop, calls=%fused_computation.174 | loop fusion | bytes 41943040 | tf_op jit(solution)/shard_map/slice | solution.py:45
  61.4 13.2 %reduce_window_sum.11 = f32[8,258,130]{1,0,2:T(8,128)S(1)} reduce-window(f32[8,258,130]{1,0,2:T(8,128)} %fusion.63, f32[]{:T(128)} %constant.177.clone.1), window={size=8x1x1 pad=7_0x0_0x0_0}, to_apply=%region_2.3 | reduce-window | flops 1878240 | bytes 2146564 | tf_op jit(solution)/shard_map/jit(cumsum)/reduce_window_sum | solution.py:50
  74.7 8.3 %multiply_add_fusion = f32[4,8,256,128]{2,1,3,0:T(8,128)S(1)} fusion(f32[4,8,256,128]{2,1,0,3:T(8,128)} %get-tuple-element.147, f32[4,8,256,128]{2,1,0,3:T(8,128)} %get-tuple-element.149, f32[4,8,256,128]{2,1,0,3:T(8,128)} %get-tuple-element.148, f32[4,8,256,128]{2,1,0,3:T(8,128)} %get-tuple-element.146, f32[4,8,256,128]{2,1,0,3:T(8,128)} %get-tuple-element.145, ...), kind=kLoop, calls=%fused_computation.137 | loop fusion | flops 14680064 | bytes 27262976 | tf_op jit(solution)/shard_map/add | solution.py:59
  86.7 15.3 %conditional.3 = (f32[4,8,128,128]{3,2,1,0:T(8,128)}) conditional(s32[]{:T(128)} %convert_element_type.11, () %tuple.31, (f32[4,8,256,128]{2,1,3,0:T(8,128)}, f32[7,256,128]{2,1,0:T(8,128)S(1)}) %tuple.105), branch_computations={%region_6.7_spmd, %region_7.8_spmd} | conditional | flops 4079615 | bytes 21757960 | solution.py:128
  86.7 5.3 %copy.40 = f32[4,8,256,128]{3,2,1,0:T(8,128)} copy(f32[4,8,256,128]{2,1,3,0:T(8,128)} %get-tuple-element.69) | data formatting | bytes 8388608 | tf_op jit(solution)/shard_map
  92.2 2.7 subtract_dynamic-update-slice_fusion.1
  102.0 15.2 %conditional.2 = (f32[4,8,128,128]{3,2,1,0:T(8,128)}) conditional(s32[]{:T(128)} %convert_element_type.10, () %tuple.29, (f32[4,8,256,128]{2,1,3,0:T(8,128)}, f32[7,256,128]{2,1,0:T(8,128)S(1)}) %tuple.106), branch_computations={%region_3.4_spmd, %region_4.5_spmd} | conditional | flops 4079615 | bytes 21757960 | solution.py:128
  102.0 5.3 %copy.39 = f32[4,8,256,128]{3,2,1,0:T(8,128)} copy(f32[4,8,256,128]{2,1,3,0:T(8,128)} %get-tuple-element.67) | data formatting | bytes 8388608 | tf_op jit(solution)/shard_map
  107.5 2.6 subtract_dynamic-update-slice_fusion
  117.1 2.6 broadcast_multiply_fusion.2
  119.8 2.7 pad_maximum_fusion.1
  122.5 3.1 collective-permute-start.10
  134.2 81.5 %collective-permute-done.10 = f32[4,8,256,128]{3,2,1,0:T(8,128)} collective-permute-done((f32[4,8,256,128]{3,2,1,0:T(8,128)}, f32[4,8,256,128]{3,2,1,0:T(8,128)}, u32[]{:S(2)}, u32[]{:S(2)}) %collective-permute-start.10) | collective-permute-done | bytes 4194336 | tf_op jit(solution)/shard_map/ppermute | solution.py:40
  215.7 92.8 %collective-permute-done.9 = f32[4,8,256,128]{3,2,1,0:T(8,128)} collective-permute-done((f32[4,8,256,128]{3,2,1,0:T(8,128)}, f32[4,8,256,128]{3,2,1,0:T(8,128)}, u32[]{:S(2)}, u32[]{:S(2)}) %collective-permute-start.9) | collective-permute-done | bytes 4194336 | tf_op jit(solution)/shard_map/ppermute | solution.py:40
  309.7 89.1 %collective-permute-done.7 = f32[4,8,256,128]{3,2,1,0:T(8,128)} collective-permute-done((f32[4,8,256,128]{3,2,1,0:T(8,128)}, f32[4,8,256,128]{3,2,1,0:T(8,128)}, u32[]{:S(2)}, u32[]{:S(2)}) %collective-permute-start.7) | collective-permute-done | bytes 4194336 | tf_op jit(solution)/shard_map/ppermute | solution.py:40
  398.7 7.4 %select_select_fusion.1 = (f32[4,8,256,128]{3,2,1,0:T(8,128)S(1)}, f32[4,8,256,128]{3,2,1,0:T(8,128)S(1)}) fusion(f32[4,8,256,128]{3,2,1,0:T(8,128)} %collective-permute-done.7, f32[4,8,256,128]{3,2,1,0:T(8,128)} %collective-permute-done.8, f32[4,8,256,128]{3,2,1,0:T(8,128)} %collective-permute-done.9, f32[4,8,256,128]{3,2,1,0:T(8,128)} %collective-permute-done.10, ...), kind=kLoop, calls=%fused_computation.136 | loop fusion | flops 9437184 | bytes 29360136 | tf_op jit(solution)/shard_map/jit(_where)/select_n | solution.py:97
  (72 shorter events, 45.5 us)
Async XLA Ops:
  9.1 1.9 copy-start.2
  15.3 6.8 %collective-permute-start.1 = (f32[4,8,1,128]{3,1,2,0:T(8,128)S(1)}, f32[4,8,1,128]{3,1,2,0:T(8,128)S(1)}, u32[]{:S(2)}, u32[]{:S(2)}) collective-permute-start(f32[4,8,1,128]{3,1,2,0:T(8,128)S(1)} %copy.30), channel_id=1, source_target_pairs={{4,0},{8,4},{12,8},{16,12},{20,16},{24,20},{28,24},{0,28},{5,1},{9... | collective-permute-start | bytes 49160 | tf_op jit(solution)/shard_map/ppermute | solution.py:25
  16.0 4.1 %collective-permute-start = (f32[4,8,1,128]{3,1,2,0:T(8,128)S(1)}, f32[4,8,1,128]{3,1,2,0:T(8,128)S(1)}, u32[]{:S(2)}, u32[]{:S(2)}) collective-permute-start(f32[4,8,1,128]{3,1,2,0:T(8,128)S(1)} %copy.29), channel_id=1, source_target_pairs={{0,4},{4,8},{8,12},{12,16},{16,20},{20,24},{24,28},{28,0},{1,5},{5... | collective-permute-start | bytes 49160 | tf_op jit(solution)/shard_map/ppermute | solution.py:23
  19.3 11.2 %collective-permute-start.4 = (f32[4,8,256]{2,1,0:T(8,128)S(1)}, f32[4,8,256]{2,1,0:T(8,128)S(1)}, u32[]{:S(2)}, u32[]{:S(2)}) collective-permute-start(f32[4,8,256]{2,1,0:T(8,128)S(1)} %slice_bitcast_fusion.3), channel_id=1, source_target_pairs={{0,4},{4,0},{8,12},{12,8},{16,20},{20,16},{24,28},{28,24},{1,5},{5... | collective-permute-start | bytes 98312 | tf_op jit(solution)/shard_map/ppermute | solution.py:35
  25.9 9.4 %collective-permute-start.2 = (f32[4,8,258,1]{2,1,0,3:T(8,128)S(1)}, f32[4,8,258,1]{2,1,0,3:T(8,128)S(1)}, u32[]{:S(2)}, u32[]{:S(2)}) collective-permute-start(f32[4,8,258,1]{2,1,0,3:T(8,128)S(1)} %get-tuple-element.141), channel_id=1, source_target_pairs={{0,1},{1,2},{2,3},{4,5},{5,6},{6,7},{8,9},{9,10},{10,11},{12,13},{... | collective-permute-start | bytes 99080 | tf_op jit(solution)/shard_map/ppermute | solution.py:23
  29.1 6.2 %collective-permute-start.3 = (f32[4,8,258,1]{2,1,0,3:T(8,128)S(1)}, f32[4,8,258,1]{2,1,0,3:T(8,128)S(1)}, u32[]{:S(2)}, u32[]{:S(2)}) collective-permute-start(f32[4,8,258,1]{2,1,0,3:T(8,128)S(1)} %get-tuple-element.142), channel_id=1, source_target_pairs={{1,0},{2,1},{3,2},{5,4},{6,5},{7,6},{9,8},{10,9},{11,10},{13,12},{... | collective-permute-start | bytes 99080 | tf_op jit(solution)/shard_map/ppermute | solution.py:25
  30.6 3.4 collective-permute-start.5
  34.0 8.6 %copy-start.5 = (f32[4]{0:T(128)S(1)}, f32[4]{0:T(128)}, u32[]{:S(2)}) copy-start(f32[4]{0:T(128)} %constant.187.clone) | copy-start | bytes 52
  34.0 8.4 %collective-permute-start.6 = (f32[4,8,256]{2,1,0:T(8,128)S(1)}, f32[4,8,256]{2,1,0:T(8,128)S(1)}, u32[]{:S(2)}, u32[]{:S(2)}) collective-permute-start(f32[4,8,256]{2,1,0:T(8,128)S(1)} %collective-permute-done.5), channel_id=1, source_target_pairs={{0,16},{4,20},{8,24},{12,28},{16,0},{20,4},{24,8},{28,12},{1,17},{... | collective-permute-start | bytes 98312 | tf_op jit(solution)/shard_map/ppermute | solution.py:35
  44.6 7.3 %copy-start = (f32[4,8,258,130]{2,1,0,3:T(8,128)S(1)}, f32[4,8,258,130]{2,1,0,3:T(8,128)}, u32[]{:S(2)}) copy-start(f32[4,8,258,130]{2,1,0,3:T(8,128)} %scatter.4) | copy-start | bytes 12879364
  61.4 13.3 %copy-start.4 = (f32[8,256,128]{1,0,2:T(8,128)S(1)}, f32[8,256,128]{1,0,2:T(8,128)}, u32[]{:S(2)}) copy-start(f32[8,256,128]{1,0,2:T(8,128)} %get-tuple-element.143) | copy-start | bytes 3145732
  84.3 2.4 copy-start.3
  119.8 2.7 copy-start.1
  119.8 8.7 %copy-start.6 = (s32[16,1]{0,1:T(1,128)S(1)}, s32[16,1]{0,1:T(1,128)}, u32[]{:S(2)}) copy-start(s32[16,1]{0,1:T(1,128)} %param.18) | copy-start | bytes 196
  122.5 93.2 %collective-permute-start.10 = (f32[4,8,256,128]{3,2,1,0:T(8,128)}, f32[4,8,256,128]{3,2,1,0:T(8,128)}, u32[]{:S(2)}, u32[]{:S(2)}) collective-permute-start(f32[4,8,256,128]{3,2,1,0:T(8,128)} %pad_maximum_fusion.1), channel_id=1, source_target_pairs={{0,4},{4,8},{8,12},{12,16},{16,20},{20,24},{24,28},{28,0},{1,5},{5... | collective-permute-start | bytes 12582920 | tf_op jit(solution)/shard_map/ppermute | solution.py:40
  125.5 183.0 %collective-permute-start.9 = (f32[4,8,256,128]{3,2,1,0:T(8,128)}, f32[4,8,256,128]{3,2,1,0:T(8,128)}, u32[]{:S(2)}, u32[]{:S(2)}) collective-permute-start(f32[4,8,256,128]{3,2,1,0:T(8,128)} %pad_maximum_fusion.1), channel_id=1, source_target_pairs={{0,8},{4,12},{8,16},{12,20},{16,24},{20,28},{24,0},{28,4},{1,9},{5... | collective-permute-start | bytes 12582920 | tf_op jit(solution)/shard_map/ppermute | solution.py:40
  128.1 181.6 %collective-permute-start.8 = (f32[4,8,256,128]{3,2,1,0:T(8,128)}, f32[4,8,256,128]{3,2,1,0:T(8,128)}, u32[]{:S(2)}, u32[]{:S(2)}) collective-permute-start(f32[4,8,256,128]{3,2,1,0:T(8,128)} %pad_maximum_fusion.1), channel_id=1, source_target_pairs={{0,28},{4,0},{8,4},{12,8},{16,12},{20,16},{24,20},{28,24},{1,29},{... | collective-permute-start | bytes 12582920 | tf_op jit(solution)/shard_map/ppermute | solution.py:40
  128.1 270.6 %collective-permute-start.7 = (f32[4,8,256,128]{3,2,1,0:T(8,128)}, f32[4,8,256,128]{3,2,1,0:T(8,128)}, u32[]{:S(2)}, u32[]{:S(2)}) collective-permute-start(f32[4,8,256,128]{3,2,1,0:T(8,128)} %pad_maximum_fusion.1), channel_id=1, source_target_pairs={{0,24},{4,28},{8,0},{12,4},{16,8},{20,12},{24,16},{28,20},{1,25},{... | collective-permute-start | bytes 12582920 | tf_op jit(solution)/shard_map/ppermute | solution.py:40
where the time goes:
time: 411 us; the launch traced here: 409 us
  waiting for transfers between devices  265 us (64%)
  other arithmetic  72.9 us (18%)
  local copies, waits for them, and re-layouts  48.2 us (12%)
  starting transfers between devices  16.9 us (4%)
  between operations  6.59 us (2%)
    ppermute x4, waiting for transfers between devices, from_behind(): lax.ppermute(value, axis, [(i, (i + by) % length) for i in range(length)])  265 us
    another operation x1, other arithmetic, tendency(): pressure = weight_coef * jnp.cumsum(density, axis=0)  13.2 us
    cond x8, other arithmetic  11.7 us
    another operation x2, local copies, waits for them, and re-layouts  10.6 us
    slice x1, local copies, waits for them, and re-layouts, tendency(): east_cells = padded[:, :, 2:, 1:-1]  9.49 us
    add x1, other arithmetic, tendency(): updated = center + advect + diffuse  8.25 us
  transfers between devices with their start and end apart: 11, of which 4 were waited for; matrix products, arithmetic and copies ran while one was open for 4% of the time, Pallas kernels for 0%

commit v1 on v0

v1 whole, which is shorter than its diff:
```python
import functools

import jax
import jax.numpy as jnp
from jax import lax
from jax.experimental import pallas as pl
from jax.experimental.pallas import tpu as pltpu
from jax.sharding import PartitionSpec as P

advect_coef = 0.1
diffuse_coef = 0.1
gradient_coef = 0.1
thermal_coef = 0.2
haline_coef = 0.15
weight_coef = 0.25

F32 = jnp.float32
MIB = 1 << 20
CHUNKS = 2


def edges_kernel(state_ref, mask_ref, lat_ref, lon_ref):
    levels, rows, lanes = state_ref.shape[1:]
    half = rows // 2
    field = pl.program_id(0)
    lane = lax.broadcasted_iota(jnp.int32, (8, lanes), 1)

    @pl.when(field == 0)
    def _():
        lat_ref[...] = jnp.zeros_like(lat_ref)

    def group(g, _):
        part = jnp.zeros((8, lanes), F32)
        for slot in range(2):
            at = pl.ds(pl.multiple_of(slot * half + g * 8, 8), 8)
            wet = mask_ref[at, :].astype(F32)
            for k in range(levels):
                x = state_ref[0, k, at, :] * wet
                place = 64 * slot + 2 * k
                part = jnp.where((lane >> 1) == (place >> 1), pltpu.roll(x, place + 1, 1), part)
        to = pl.ds(pl.multiple_of(g * 8, 8), 8)
        lat_ref[to, :] += pltpu.roll(part, field * (2 * levels), 1)
        return 0

    lax.fori_loop(0, half // 8, group, 0)
    for k in range(levels):
        lon_ref[0, k : k + 1, :] = state_ref[0, k, 0:1, :] * mask_ref[0:1, :].astype(F32)
        lon_ref[1, k : k + 1, :] = (
            state_ref[0, k, rows - 1 : rows, :] * mask_ref[rows - 1 : rows, :].astype(F32)
        )


def edges(state, mask):
    fields, levels, rows, lanes = state.shape
    return pl.pallas_call(
        edges_kernel,
        grid=(fields,),
        in_specs=[
            pl.BlockSpec((1, levels, rows, lanes), lambda f: (f, 0, 0, 0)),
            pl.BlockSpec((rows, lanes), lambda f: (0, 0)),
        ],
        out_specs=[
            pl.BlockSpec((rows // 2, lanes), lambda f: (0, 0)),
            pl.BlockSpec((2, levels, lanes), lambda f: (0, f, 0)),
        ],
        out_shape=[
            jax.ShapeDtypeStruct((rows // 2, lanes), F32),
            jax.ShapeDtypeStruct((2, fields * levels, lanes), F32),
        ],
        compiler_params=pltpu.CompilerParams(vmem_limit_bytes=24 * MIB),
    )(state, mask)


def step_kernel(
    state_ref, diff_ref, mask_ref, north_ref, south_ref, west_ref, east_ref, theirs_ref, mine_ref, padded
):
    fields, levels, rows, lanes = state_ref.shape
    quarter = rows // 4
    at_step = pl.program_id(0)
    core = lax.rem(lax.axis_index("lon"), 2)
    lane = lax.broadcasted_iota(jnp.int32, (8, lanes), 1)

    @pl.when(at_step == 0)
    def _():
        def fill(g, _):
            at = pl.ds(pl.multiple_of(g * 8, 8), 8)
            to = pl.ds(pl.multiple_of(g * 8 + 8, 8), 8)
            wet = mask_ref[at, :].astype(F32)
            for f in range(fields):
                for k in range(levels):
                    padded[f, k, to, :] = state_ref[f, k, at, :] * wet
            return 0

        lax.fori_loop(0, rows // 8, fill, 0)
        for f in range(fields):
            for k in range(levels):
                i = f * levels + k
                padded[f, k, 7:8, :] = west_ref[i : i + 1, :]
                padded[f, k, rows + 8 : rows + 9, :] = east_ref[i : i + 1, :]

    slot = lax.rem(at_step, 2)
    half = jnp.where(at_step < 2, 1 - core, core)
    is_last = lane == lanes - 1
    is_first = lane == 0

    def make(out_ref):
        def group(g, _):
            row = pl.multiple_of(half * quarter + g * 8, 8)
            base = pl.multiple_of(slot * (2 * quarter) + row, 8)
            north_pack = pltpu.roll(north_ref[pl.ds(row, 8), :], 64 * slot, 1)
            south_pack = pltpu.roll(south_ref[pl.ds(row, 8), :], 64 * slot, 1)
            wet = mask_ref[pl.ds(base, 8), :].astype(F32)
            zonal = meridional = None
            carry = None
            upper = []
            rhs = []
            for k in range(levels):
                center = [padded[f, k, pl.ds(base + 8, 8), :] for f in range(fields)]
                grad_x, grad_y, total = [], [], []
                for f in range(fields):
                    i = f * levels + k
                    e = padded[f, k, pl.ds(base + 9, 8), :]
                    w = padded[f, k, pl.ds(base + 7, 8), :]
                    n = jnp.where(
                        is_last,
                        pltpu.roll(north_pack, (lanes - 1 - (2 * i + 1)) % lanes, 1),
                        pltpu.roll(center[f], lanes - 1, 1),
                    )
                    s = jnp.where(
                        is_first,
                        pltpu.roll(south_pack, (lanes - 2 * i) % lanes, 1),
                        pltpu.roll(center[f], 1, 1),
                    )
                    grad_x.append(e - w)
                    grad_y.append(n - s)
                    total.append((e + w) + (n + s))
                dx = haline_coef * grad_x[1] - thermal_coef * grad_x[0]
                dy = haline_coef * grad_y[1] - thermal_coef * grad_y[0]
                zonal = dx if k == 0 else zonal + dx
                meridional = dy if k == 0 else meridional + dy
                u, v = center[2], center[3]
                lower_k = diff_ref[k - 1, pl.ds(base, 8), :] if k > 0 else None
                upper_k = diff_ref[k, pl.ds(base, 8), :] if k < levels - 1 else None
                pivot = 1.0
                if k > 0:
                    pivot = pivot + lower_k
                if k < levels - 1:
                    pivot = pivot + upper_k
                if k > 0:
                    pivot = pivot - lower_k * upper[k - 1]
                inverse = 1.0 / pivot
                upper.append(upper_k * inverse if k < levels - 1 else None)
                row_rhs = []
                for f in range(fields):
                    flow = u * grad_x[f] + v * grad_y[f]
                    value = (1.0 - 4.0 * diffuse_coef) * center[f] + (
                        diffuse_coef * total[f] - advect_coef * flow
                    )
                    if f == 2:
                        value = value - (gradient_coef * weight_coef) * zonal
                    if f == 3:
                        value = value - (gradient_coef * weight_coef) * meridional
                    if k > 0:
                        value = value + lower_k * rhs[k - 1][f]
                    row_rhs.append(value * inverse)
                rhs.append(row_rhs)
            to = pl.ds(pl.multiple_of(g * 8, 8), 8)
            for f in range(fields):
                x = rhs[levels - 1][f]
                out_ref[0, f, levels - 1, to, :] = x * wet
                for k in range(levels - 2, -1, -1):
                    x = rhs[k][f] + upper[k] * x
                    out_ref[0, f, k, to, :] = x * wet
            return 0

        lax.fori_loop(0, quarter // 8, group, 0)

    @pl.when(at_step < 2)
    def _():
        make(theirs_ref)

    @pl.when(at_step >= 2)
    def _():
        make(mine_ref)


def step(state, diffusivity, mask, north, south, west, east):
    fields, levels, rows, lanes = state.shape
    whole = lambda a: pl.BlockSpec(a.shape, lambda i, nd=a.ndim: (0,) * nd)
    block = (1, fields, levels, rows // 4, lanes)
    shape = jax.ShapeDtypeStruct((2, fields, levels, rows // 4, lanes), F32)
    return pl.pallas_call(
        step_kernel,
        grid=(4,),
        in_specs=[whole(a) for a in (state, diffusivity, mask, north, south, west, east)],
        out_specs=[
            pl.BlockSpec(block, lambda i: (jnp.minimum(i, 1), 0, 0, 0, 0)),
            pl.BlockSpec(block, lambda i: (jnp.maximum(i - 2, 0), 0, 0, 0, 0)),
        ],
        out_shape=[shape, shape],
        scratch_shapes=[pltpu.VMEM((fields, levels, rows + 16, lanes), F32)],
        compiler_params=pltpu.CompilerParams(vmem_limit_bytes=40 * MIB),
    )(state, diffusivity, mask, north, south, west, east)


def chip_of():
    return lax.axis_index("lon") // 2, lax.rem(lax.axis_index("lon"), 2)


def leaves(plan_ref, chips, chip, t, way):
    target = plan_ref[4 * chip + t] // 4
    return target == lax.rem(chip + way + chips, chips)


def pack_kernel(rounds, chips, plan_ref, mine, other, *rest):
    outs, sem = rest[:-1], rest[-1]
    chip, core = chip_of()
    fields = mine.shape[1]
    span = fields // CHUNKS
    at = 0
    jobs = []
    for way in (1, -1):
        for r in range(rounds):
            count = jnp.int32(0)
            chosen = jnp.int32(0)
            for t in range(4):
                hit = leaves(plan_ref, chips, chip, t, way)
                chosen = jnp.where(hit & (count == r), t, chosen)
                count = count + hit.astype(jnp.int32)
            jobs.append((way, r, chosen))
    for chunk in range(CHUNKS):
        for way, r, chosen in jobs:
            out = outs[chunk * 2 + (0 if way == 1 else 1)]
            own = chosen // 2 == core
            slot = lax.rem(chosen, 2)
            for is_own, source in ((True, mine), (False, other)):
                copy = pltpu.make_async_copy(
                    source.at[slot, pl.ds(chunk * span, span)], out.at[r], sem.at[at]
                )
                pl.when(own if is_own else jnp.logical_not(own))(copy.start)
            at += 1
    at = 0
    for chunk in range(CHUNKS):
        for way, r, chosen in jobs:
            out = outs[chunk * 2 + (0 if way == 1 else 1)]
            pltpu.make_async_copy(mine.at[0, pl.ds(chunk * span, span)], out.at[r], sem.at[at]).wait()
            at += 1


def place_kernel(rounds, chips, plan_ref, *rest):
    mine, theirs, other, other_theirs = rest[:4]
    arrived = rest[4:-2]
    out, sem = rest[-2:]
    chip, core = chip_of()
    fields, quarter = mine.shape[1], mine.shape[3]
    span = fields // CHUNKS
    tiles = 4 * chips
    waits = []
    for slot in range(2):
        target = 2 * lax.axis_index("lon") + slot
        source = jnp.int32(0)
        for shift in range(-3, 4):
            g = lax.rem(target + shift + tiles, tiles)
            source = jnp.where(plan_ref[g] == target, g, source)
        from_chip = source // 4
        t = lax.rem(source, 4)
        local = from_chip == chip
        own = t // 2 == core
        tslot = lax.rem(t, 2)
        for part in range(2):
            half = core if part == 0 else 1 - core
            row = pl.multiple_of(2 * quarter * slot + half * quarter, quarter)
            for chunk in range(CHUNKS):
                where_f = pl.ds(chunk * span, span)
                to = out.at[where_f, :, pl.ds(row, quarter), :]
                s = sem.at[(slot * 2 + part) * CHUNKS + chunk]
                held = mine if part == 0 else theirs
                held_other = other if part == 0 else other_theirs
                pl.when(local & own)(
                    pltpu.make_async_copy(held.at[tslot, where_f], to, s).start
                )
                pl.when(local & jnp.logical_not(own))(
                    pltpu.make_async_copy(held_other.at[tslot, where_f], to, s).start
                )
                for side, way in enumerate((1, -1)):
                    came = from_chip == lax.rem(chip - way + chips, chips)
                    rank = jnp.int32(0)
                    for q in range(3):
                        hit = leaves(plan_ref, chips, from_chip, q, way) & (q < t)
                        rank = rank + hit.astype(jnp.int32)
                    rank = jnp.minimum(rank, rounds - 1)
                    buffer = arrived[(part * CHUNKS + chunk) * 2 + side]
                    pl.when(came)(pltpu.make_async_copy(buffer.at[rank], to, s).start)
                waits.append((held.at[0, where_f], to, s))
    for a, b, s in waits:
        pltpu.make_async_copy(a, b, s).wait()


def exchange(rounds, plan, mine, theirs, other):
    devices = lax.axis_size("lon")
    chips = devices // 2
    fields, levels, quarter, lanes = mine.shape[1:]
    span = fields // CHUNKS
    swap = [(i, i ^ 1) for i in range(devices)]
    anywhere = pl.BlockSpec(memory_space=pl.ANY)
    scalars = pl.BlockSpec(memory_space=pltpu.SMEM)
    piece = jax.ShapeDtypeStruct((rounds, span, levels, quarter, lanes), F32)
    sends = pl.pallas_call(
        functools.partial(pack_kernel, rounds, chips),
        in_specs=[scalars, anywhere, anywhere],
        out_specs=[anywhere] * (2 * CHUNKS),
        out_shape=[piece] * (2 * CHUNKS),
        scratch_shapes=[pltpu.SemaphoreType.DMA((2 * CHUNKS * rounds,))],
    )(plan, mine, other)
    arrived = []
    for at, send in enumerate(sends):
        by = 2 if at % 2 == 0 else -2
        arrived.append(lax.ppermute(send, "lon", [(i, (i + by) % devices) for i in range(devices)]))
    other_theirs = lax.ppermute(mine, "lon", swap)
    swapped = [lax.ppermute(a, "lon", swap) for a in arrived]
    return pl.pallas_call(
        functools.partial(place_kernel, rounds, chips),
        in_specs=[scalars] + [anywhere] * (4 + 4 * CHUNKS),
        out_specs=anywhere,
        out_shape=jax.ShapeDtypeStruct((fields, levels, 4 * quarter, lanes), F32),
        scratch_shapes=[pltpu.SemaphoreType.DMA((4 * CHUNKS,))],
    )(plan, mine, theirs, other, other_theirs, *arrived, *swapped)


def most_rounds(plan, chips):
    target = (plan // 4).reshape(chips, 4)
    home = jnp.arange(chips, dtype=jnp.int32)[:, None]
    apart = jnp.mod(target - home, chips)
    east = jnp.max(jnp.sum((apart == 1).astype(jnp.int32), axis=1))
    west = jnp.max(jnp.sum((apart == chips - 1).astype(jnp.int32), axis=1))
    most = jnp.maximum(east, west)
    rows = lax.axis_size("lat")
    apart = 1
    while apart < rows:
        most = jnp.maximum(most, lax.ppermute(most, "lat", [(i, i ^ apart) for i in range(rows)]))
        apart *= 2
    return most


def local(state, diffusivity, mask, tile_plan):
    devices, bands = lax.axis_size("lon"), lax.axis_size("lat")
    plan = tile_plan.reshape(-1)
    most = most_rounds(plan, devices // 2)
    lat_pack, lon_pack = edges(state, mask)
    fold = lax.ppermute(
        lat_pack,
        ("lon", "lat"),
        [(i * bands + bands - 1, (devices - 1 - i) * bands + bands - 1) for i in range(devices)],
    )
    above = lax.ppermute(lat_pack, "lat", [(i + 1, i) for i in range(bands - 1)])
    south = lax.ppermute(lat_pack, "lat", [(i, i + 1) for i in range(bands - 1)])
    west = lax.ppermute(lon_pack[1], "lon", [(i, (i + 1) % devices) for i in range(devices)])
    east = lax.ppermute(lon_pack[0], "lon", [((i + 1) % devices, i) for i in range(devices)])
    lanes = state.shape[3]
    sign = jnp.where(jnp.arange(lanes) % 64 >= 32, -1.0, 1.0).astype(F32)
    mirror = jnp.roll(fold[::-1], 65, axis=1) * sign
    north = jnp.where(lax.axis_index("lat") == bands - 1, mirror, above)
    theirs, mine = step(state, diffusivity, mask, north, south, west, east)
    other = lax.ppermute(theirs, "lon", [(i, i ^ 1) for i in range(devices)])
    branches = [functools.partial(exchange, rounds) for rounds in (1, 2, 3)]
    return lax.switch(jnp.clip(most - 1, 0, 2), branches, plan, mine, theirs, other)


def solution(mesh):
    placed = (P(None, None, "lon", "lat"), P(None, "lon", "lat"), P("lon", "lat"), P(None, "lat"))
    return jax.shard_map(
        local, mesh=mesh, in_specs=placed, out_specs=P(None, None, "lon", "lat"), check_vma=False
    )
```

time: 411 us -> 280 us (0.68)
  waiting for transfers between devices: 265 us -> 7.4 us
  Pallas kernels: 0 us -> 152 us
  starting transfers between devices: 16.9 us -> 108 us
  other arithmetic: 72.9 us -> 2.21 us
  local copies, waits for them, and re-layouts: 48.2 us -> 6.79 us
    ppermute x11 -> x17, waiting for transfers between devices: 265 us -> 7.4 us  [the longest x4 4.42 us: exchange(): lax.ppermute(send, 'lon', [(i, (i + by) % devices) for i in range(devices)])]
    pallas_call x0 -> x4, Pallas kernels: none -> 152 us  [the longest x1 129 us: exchange(): pl.pallas_call(functools.partial(place_kernel, rounds, chips), in_specs=[...]
    ppermute x11 -> x17, starting transfers between devices: 16.9 us -> 108 us  [the longest x4 81.3 us: exchange(): swapped = [lax.ppermute(a, 'lon', swap) for a in arrived]]
    another operation x4 -> x0, other arithmetic: 16.7 us -> none  [the longest x1 13.2 us: tendency(): pressure = weight_coef * jnp.cumsum(density, axis=0)]
    slice x4 -> x3, local copies, waits for them, and re-layouts: 14.4 us -> 0.1 us  [local(): mirror = jnp.roll(fold[::-1], 65, axis=1) * sign]
    concatenate x3 -> x0, other arithmetic: 12.2 us -> none  [the longest x1 7.08 us: extended(): jnp.concatenate([lax.ppermute(tail, axis, [(i, (i + 1) % count) for i in...]
    cond x8 -> x0, other arithmetic: 11.7 us -> none
    another operation x2 -> x0, local copies, waits for them, and re-layouts: 10.6 us -> none
  transfers between devices with their start and end apart: 11 -> 17, of which waited for: 4 -> 6; matrix products, arithmetic and copies ran while one was open for 4% -> 1% of each run, Pallas kernels for 0% -> 1%
where the time goes in v1:
time: 280 us; the launch traced here: 279 us
  Pallas kernels  152 us (54%)
  starting transfers between devices  108 us (39%)
  waiting for transfers between devices  7.4 us (3%)
  local copies, waits for them, and re-layouts  6.79 us (2%)
    pallas_call x1, Pallas kernels, exchange(): pl.pallas_call(functools.partial(place_kernel, rounds, chips), in_specs=[...  129 us
    ppermute x4, starting transfers between devices, exchange(): swapped = [lax.ppermute(a, 'lon', swap) for a in arrived]  81.3 us
    pallas_call x1, Pallas kernels, step(): pl.pallas_call(step_kernel, grid=(4,), in_specs=[whole(a) for a in (state...  11.3 us
    pallas_call x1, Pallas kernels, edges(): pl.pallas_call(edges_kernel, grid=(fields,), in_specs=[pl.BlockSpec((1, l...  9.99 us
    ppermute x2, starting transfers between devices, most_rounds(): lax.ppermute(most, 'lat', [(i, i ^ apart) for i in range(rows)])  8.53 us
    unnamed x13, local copies, waits for them, and re-layouts  5.8 us
  transfers between devices with their start and end apart: 17, of which 6 were waited for; matrix products, arithmetic and copies ran while one was open for 1% of the time, Pallas kernels for 1%

profile of v1, /device:TPU:1, one launch (start us, length us, event | category | flops | bytes accessed | tf_op | source)
XLA Modules:
  0.0 279.3 jit_solution(5035671555027995136)
XLA Ops:
  0.0 2.2 copy-done
  2.2 0.9 copy-done.3
  3.1 10.0 %shard_map.49 = (f32[128,128]{1,0:T(8,128)S(1)}, f32[2,32,128]{2,1,0:T(8,128)S(1)}) custom-call(f32[4,8,256,128]{3,2,1,0:T(8,128)S(1)} %copy-done, s32[256,128]{1,0:T(8,128)S(1)} %copy-done.3), custom_call_target="tpu_custom_call" | custom-call | tf_op jit(solution)/shard_map/pallas_call | solution.py:55
  13.1 4.0 %collective-permute-start.31 = (f32[128,128]{1,0:T(8,128)S(1)}, f32[128,128]{1,0:T(8,128)S(1)}, u32[]{:S(2)}, u32[]{:S(2)}) collective-permute-start(f32[128,128]{1,0:T(8,128)S(1)} %get-tuple-element.61), channel_id=1, source_target_pairs={{0,1},{1,2},{2,3},{4,5},{5,6},{6,7},{8,9},{9,10},{10,11},{12,13},{... | collective-permute-start | bytes 196616 | tf_op jit(solution)/shard_map/ppermute | solution.py:356
  17.1 1.3 collective-permute-start.30
  19.1 1.0 collective-permute-start.33
  20.1 1.2 collective-permute-start.32
  22.7 2.2 copy-done.1
  24.9 11.3 %shard_map.50 = (f32[2,4,8,64,128]{4,3,2,1,0:T(8,128)}, f32[2,4,8,64,128]{4,3,2,1,0:T(8,128)S(1)}) custom-call(f32[4,8,256,128]{3,2,1,0:T(8,128)S(1)} %copy-done.1, f32[7,256,128]{2,1,0:T(8,128)S(1)} %copy-done.2, s32[256,128]{1,0:T(8,128)S(1)} %copy-done.4, f32[128,128]{1,0:T(8,128)S(1)} %fusion.north_ref, ...), custom_call_target="tpu_custom_call" | custom-call | tf_op jit(solution)/shard_map/pallas_call | solution.py:192
  36.1 3.1 %collective-permute-start.34 = (f32[2,4,8,64,128]{4,3,2,1,0:T(8,128)}, f32[2,4,8,64,128]{4,3,2,1,0:T(8,128)}, u32[]{:S(2)}, u32[]{:S(2)}) collective-permute-start(f32[2,4,8,64,128]{4,3,2,1,0:T(8,128)} %get-tuple-element.64), channel_id=1, source_target_pairs={{0,4},{4,0},{8,12},{12,8},{16,20},{20,16},{24,28},{28,24},{1,5},{5... | collective-permute-start | bytes 6291464 | tf_op jit(solution)/shard_map/ppermute | solution.py:364
  43.3 2.9 %collective-permute-start.27 = (s32[]{:T(128)}, s32[]{:T(128)}, u32[]{:S(2)}, u32[]{:S(2)}) collective-permute-start(s32[]{:T(128)} %max.13), channel_id=1, source_target_pairs={{0,1},{1,0},{2,3},{3,2},{4,5},{5,4},{6,7},{7,6},{8,9},{9,8},{10,11... | collective-permute-start | bytes 20 | tf_op jit(solution)/shard_map/ppermute | solution.py:340
  46.9 5.7 %collective-permute-start.28 = (s32[]{:T(128)}, s32[]{:T(128)}, u32[]{:S(2)}, u32[]{:S(2)}) collective-permute-start(s32[]{:T(128)} %max.14), channel_id=1, source_target_pairs={{0,2},{1,3},{2,0},{3,1},{4,6},{5,7},{6,4},{7,5},{8,10},{9,11},{10,... | collective-permute-start | bytes 20 | tf_op jit(solution)/shard_map/ppermute | solution.py:340
  53.4 225.9 %conditional.1 = (f32[4,8,256,128]{3,2,1,0:T(8,128)}) conditional(s32[]{:T(128)} %clamp.3, (f32[2,4,8,64,128]{4,3,2,1,0:T(8,128)S(1)}, s32[16,1]{0,1:T(1,128)S(1)}, f32[2,4,8,64,128]{4,3,2,1,0:T(8,128)}, f32[2,4,8,64,128]{4,3,2,1,0:T(8,128)}) %tuple.23, (f32[2,4,8,64,128]{4,3,2,1,0:T(8,128)S(1)}, s32[16,1]{0,1:T(1,128)S(1)}, ...), branch_computations={%region_4.5_spmd, %region_5.6_spmd, %region_6.7_spmd} | conditional | bytes 117441120 | solution.py:366
  53.4 2.1 collective-permute-start
  55.5 2.0 branch_0_fun.2
  58.0 2.0 collective-permute-start.2
  60.1 2.3 collective-permute-start.4
  62.4 4.4 %collective-permute-done.1.rest_4_ = f32[1,2,8,64,128]{4,3,2,1,0:T(8,128)S(1)} collective-permute-done((f32[1,2,8,64,128]{4,3,2,1,0:T(8,128)}, f32[1,2,8,64,128]{4,3,2,1,0:T(8,128)S(1)}, u32[]{:S(2)}, u32[]{:S(2)}) %collective-permute-start.1) | collective-permute-done | bytes 524320 | tf_op jit(solution)/shard_map/cond/branch_0_fun/ppermute | solution.py:318
  66.8 64.4 %collective-permute-start.5 = (f32[1,2,8,64,128]{4,3,2,1,0:T(8,128)S(1)}, f32[1,2,8,64,128]{4,3,2,1,0:T(8,128)S(1)}, u32[]{:S(2)}, u32[]{:S(2)}) collective-permute-start(f32[1,2,8,64,128]{4,3,2,1,0:T(8,128)S(1)} %collective-permute-done.1.rest_4_), channel_id=1, source_target_pairs={{0,4},{4,0},{8,12},{12,8},{16,20},{20,16},{24,28},{28,24},{1,5},{5... | collective-permute-start | bytes 1572872 | tf_op jit(solution)/shard_map/cond/branch_0_fun/ppermute | solution.py:320
  131.2 5.7 %collective-permute-start.6 = (f32[1,2,8,64,128]{4,3,2,1,0:T(8,128)S(1)}, f32[1,2,8,64,128]{4,3,2,1,0:T(8,128)S(1)}, u32[]{:S(2)}, u32[]{:S(2)}) collective-permute-start(f32[1,2,8,64,128]{4,3,2,1,0:T(8,128)S(1)} %collective-permute-done.2.rest_5_), channel_id=1, source_target_pairs={{0,4},{4,0},{8,12},{12,8},{16,20},{20,16},{24,28},{28,24},{1,5},{5... | collective-permute-start | bytes 1572872 | tf_op jit(solution)/shard_map/cond/branch_0_fun/ppermute | solution.py:320
  136.9 5.6 %collective-permute-start.7 = (f32[1,2,8,64,128]{4,3,2,1,0:T(8,128)S(1)}, f32[1,2,8,64,128]{4,3,2,1,0:T(8,128)S(1)}, u32[]{:S(2)}, u32[]{:S(2)}) collective-permute-start(f32[1,2,8,64,128]{4,3,2,1,0:T(8,128)S(1)} %collective-permute-done.3.rest_6_), channel_id=1, source_target_pairs={{0,4},{4,0},{8,12},{12,8},{16,20},{20,16},{24,28},{28,24},{1,5},{5... | collective-permute-start | bytes 1572872 | tf_op jit(solution)/shard_map/cond/branch_0_fun/ppermute | solution.py:320
  142.4 5.7 %collective-permute-start.8 = (f32[1,2,8,64,128]{4,3,2,1,0:T(8,128)S(1)}, f32[1,2,8,64,128]{4,3,2,1,0:T(8,128)S(1)}, u32[]{:S(2)}, u32[]{:S(2)}) collective-permute-start(f32[1,2,8,64,128]{4,3,2,1,0:T(8,128)S(1)} %collective-permute-done.4.rest_7_), channel_id=1, source_target_pairs={{0,4},{4,0},{8,12},{12,8},{16,20},{20,16},{24,28},{28,24},{1,5},{5... | collective-permute-start | bytes 1572872 | tf_op jit(solution)/shard_map/cond/branch_0_fun/ppermute | solution.py:320
  148.1 1.5 collective-permute-done.8.rest_11_
  150.4 128.8 %branch_0_fun.3 = f32[4,8,256,128]{3,2,1,0:T(8,128)} custom-call(s32[16]{0:T(128)S(1)} %bitcast.11, f32[2,4,8,64,128]{4,3,2,1,0:T(8,128)S(1)} %get-tuple-element.34.mine.rest_0_, f32[2,4,8,64,128]{4,3,2,1,0:T(8,128)} %get-tuple-element.35.rest_1_, f32[2,4,8,64,128]{4,3,2,1,0:T(8,128)} %get-tuple-element.36.other.rest_2_, ...), custom_call_target="tpu_custom_call" | custom-call | tf_op jit(solution)/shard_map/cond/branch_0_fun/pallas_call | solution.py:321
  (55 shorter events, 6.4 us)
Async XLA Ops:
  3.1 19.6 %copy-start.2 = (f32[7,256,128]{2,1,0:T(8,128)S(1)}, f32[7,256,128]{2,1,0:T(8,128)}, u32[]{:S(2)}) copy-start(f32[7,256,128]{2,1,0:T(8,128)} %diff_ref.1) | copy-start | bytes 2752516
  3.1 19.6 %copy-start.4 = (s32[256,128]{1,0:T(8,128)S(1)}, s32[256,128]{1,0:T(8,128)}, u32[]{:S(2)}) copy-start(s32[256,128]{1,0:T(8,128)} %mask_ref.3) | copy-start | bytes 393220
  13.1 9.6 %collective-permute-start.31 = (f32[128,128]{1,0:T(8,128)S(1)}, f32[128,128]{1,0:T(8,128)S(1)}, u32[]{:S(2)}, u32[]{:S(2)}) collective-permute-start(f32[128,128]{1,0:T(8,128)S(1)} %get-tuple-element.61), channel_id=1, source_target_pairs={{0,1},{1,2},{2,3},{4,5},{5,6},{6,7},{8,9},{9,10},{10,11},{12,13},{... | collective-permute-start | bytes 196616 | tf_op jit(solution)/shard_map/ppermute | solution.py:356
  17.1 5.0 %collective-permute-start.30 = (f32[128,128]{1,0:T(8,128)S(1)}, f32[128,128]{1,0:T(8,128)S(1)}, u32[]{:S(2)}, u32[]{:S(2)}) collective-permute-start(f32[128,128]{1,0:T(8,128)S(1)} %get-tuple-element.61), channel_id=1, source_target_pairs={{1,0},{2,1},{3,2},{5,4},{6,5},{7,6},{9,8},{10,9},{11,10},{13,12},{... | collective-permute-start | bytes 196616 | tf_op jit(solution)/shard_map/ppermute | solution.py:355
  18.4 2.9 %collective-permute-start.29 = (f32[128,128]{1,0:T(8,128)S(1)}, f32[128,128]{1,0:T(8,128)S(1)}, u32[]{:S(2)}, u32[]{:S(2)}) collective-permute-start(f32[128,128]{1,0:T(8,128)S(1)} %get-tuple-element.61), channel_id=1, source_target_pairs={{3,31},{7,27},{11,23},{15,19},{19,15},{23,11},{27,7},{31,3}} | collective-permute-start | bytes 196616 | tf_op jit(solution)/shard_map/ppermute | solution.py:350
  19.1 3.5 %collective-permute-start.33 = (f32[32,128]{1,0:T(8,128)S(1)}, f32[32,128]{1,0:T(8,128)S(1)}, u32[]{:S(2)}, u32[]{:S(2)}) collective-permute-start(f32[32,128]{1,0:T(8,128)S(1)} %get-tuple-element.71), channel_id=1, source_target_pairs={{4,0},{8,4},{12,8},{16,12},{20,16},{24,20},{28,24},{0,28},{5,1},{9... | collective-permute-start | bytes 49160 | tf_op jit(solution)/shard_map/ppermute | solution.py:358
  20.1 2.5 collective-permute-start.32
  22.1 17.6 %copy-start.30 = (s32[16,1]{0,1:T(1,128)S(1)}, s32[16,1]{0,1:T(1,128)}, u32[]{:S(2)}) copy-start(s32[16,1]{0,1:T(1,128)} %param.10) | copy-start | bytes 196
  36.1 17.3 %collective-permute-start.34 = (f32[2,4,8,64,128]{4,3,2,1,0:T(8,128)}, f32[2,4,8,64,128]{4,3,2,1,0:T(8,128)}, u32[]{:S(2)}, u32[]{:S(2)}) collective-permute-start(f32[2,4,8,64,128]{4,3,2,1,0:T(8,128)} %get-tuple-element.64), channel_id=1, source_target_pairs={{0,4},{4,0},{8,12},{12,8},{16,20},{20,16},{24,28},{28,24},{1,5},{5... | collective-permute-start | bytes 6291464 | tf_op jit(solution)/shard_map/ppermute | solution.py:364
  43.3 3.0 %collective-permute-start.27 = (s32[]{:T(128)}, s32[]{:T(128)}, u32[]{:S(2)}, u32[]{:S(2)}) collective-permute-start(s32[]{:T(128)} %max.13), channel_id=1, source_target_pairs={{0,1},{1,0},{2,3},{3,2},{4,5},{5,4},{6,7},{7,6},{8,9},{9,8},{10,11... | collective-permute-start | bytes 20 | tf_op jit(solution)/shard_map/ppermute | solution.py:340
  46.9 5.8 %collective-permute-start.28 = (s32[]{:T(128)}, s32[]{:T(128)}, u32[]{:S(2)}, u32[]{:S(2)}) collective-permute-start(s32[]{:T(128)} %max.14), channel_id=1, source_target_pairs={{0,2},{1,3},{2,0},{3,1},{4,6},{5,7},{6,4},{7,5},{8,10},{9,11},{10,... | collective-permute-start | bytes 20 | tf_op jit(solution)/shard_map/ppermute | solution.py:340
  53.4 96.2 %collective-permute-start = (f32[2,4,8,64,128]{4,3,2,1,0:T(8,128)S(1)}, f32[2,4,8,64,128]{4,3,2,1,0:T(8,128)}, u32[]{:S(2)}, u32[]{:S(2)}) collective-permute-start(f32[2,4,8,64,128]{4,3,2,1,0:T(8,128)S(1)} %get-tuple-element.34.mine.rest_0_), channel_id=1, source_target_pairs={{0,4},{4,0},{8,12},{12,8},{16,20},{20,16},{24,28},{28,24},{1,5},{5... | collective-permute-start | bytes 6291464 | tf_op jit(solution)/shard_map/cond/branch_0_fun/ppermute | solution.py:319
  57.6 9.2 %collective-permute-start.1 = (f32[1,2,8,64,128]{4,3,2,1,0:T(8,128)}, f32[1,2,8,64,128]{4,3,2,1,0:T(8,128)S(1)}, u32[]{:S(2)}, u32[]{:S(2)}) collective-permute-start(f32[1,2,8,64,128]{4,3,2,1,0:T(8,128)} %get-tuple-element.37), channel_id=1, source_target_pairs={{0,8},{4,12},{8,16},{12,20},{16,24},{20,28},{24,0},{28,4},{1,9},{5... | collective-permute-start | bytes 1572872 | tf_op jit(solution)/shard_map/cond/branch_0_fun/ppermute | solution.py:318
  58.0 73.2 %collective-permute-start.2 = (f32[1,2,8,64,128]{4,3,2,1,0:T(8,128)}, f32[1,2,8,64,128]{4,3,2,1,0:T(8,128)S(1)}, u32[]{:S(2)}, u32[]{:S(2)}) collective-permute-start(f32[1,2,8,64,128]{4,3,2,1,0:T(8,128)} %get-tuple-element.38), channel_id=1, source_target_pairs={{0,24},{4,28},{8,0},{12,4},{16,8},{20,12},{24,16},{28,20},{1,25},{... | collective-permute-start | bytes 1572872 | tf_op jit(solution)/shard_map/cond/branch_0_fun/ppermute | solution.py:318
  60.0 76.9 %collective-permute-start.3 = (f32[1,2,8,64,128]{4,3,2,1,0:T(8,128)}, f32[1,2,8,64,128]{4,3,2,1,0:T(8,128)S(1)}, u32[]{:S(2)}, u32[]{:S(2)}) collective-permute-start(f32[1,2,8,64,128]{4,3,2,1,0:T(8,128)} %get-tuple-element.39), channel_id=1, source_target_pairs={{0,8},{4,12},{8,16},{12,20},{16,24},{20,28},{24,0},{28,4},{1,9},{5... | collective-permute-start | bytes 1572872 | tf_op jit(solution)/shard_map/cond/branch_0_fun/ppermute | solution.py:318
  60.1 82.4 %collective-permute-start.4 = (f32[1,2,8,64,128]{4,3,2,1,0:T(8,128)}, f32[1,2,8,64,128]{4,3,2,1,0:T(8,128)S(1)}, u32[]{:S(2)}, u32[]{:S(2)}) collective-permute-start(f32[1,2,8,64,128]{4,3,2,1,0:T(8,128)} %get-tuple-element.40), channel_id=1, source_target_pairs={{0,24},{4,28},{8,0},{12,4},{16,8},{20,12},{24,16},{28,20},{1,25},{... | collective-permute-start | bytes 1572872 | tf_op jit(solution)/shard_map/cond/branch_0_fun/ppermute | solution.py:318
  66.8 83.7 %copy-start.22 = (f32[1,2,8,64,128]{4,3,2,1,0:T(8,128)}, f32[1,2,8,64,128]{4,3,2,1,0:T(8,128)S(1)}, u32[]{:S(2)}) copy-start(f32[1,2,8,64,128]{4,3,2,1,0:T(8,128)S(1)} %collective-permute-done.1.rest_4_) | copy-start | bytes 1572868 | tf_op jit(solution)/shard_map/cond
  66.8 81.3 %collective-permute-start.5 = (f32[1,2,8,64,128]{4,3,2,1,0:T(8,128)S(1)}, f32[1,2,8,64,128]{4,3,2,1,0:T(8,128)S(1)}, u32[]{:S(2)}, u32[]{:S(2)}) collective-permute-start(f32[1,2,8,64,128]{4,3,2,1,0:T(8,128)S(1)} %collective-permute-done.1.rest_4_), channel_id=1, source_target_pairs={{0,4},{4,0},{8,12},{12,8},{16,20},{20,16},{24,28},{28,24},{1,5},{5... | collective-permute-start | bytes 1572872 | tf_op jit(solution)/shard_map/cond/branch_0_fun/ppermute | solution.py:320
  131.2 19.3 %copy-start.23 = (f32[1,2,8,64,128]{4,3,2,1,0:T(8,128)}, f32[1,2,8,64,128]{4,3,2,1,0:T(8,128)S(1)}, u32[]{:S(2)}) copy-start(f32[1,2,8,64,128]{4,3,2,1,0:T(8,128)S(1)} %collective-permute-done.2.rest_5_) | copy-start | bytes 1572868 | tf_op jit(solution)/shard_map/cond
  131.2 16.9 %collective-permute-start.6 = (f32[1,2,8,64,128]{4,3,2,1,0:T(8,128)S(1)}, f32[1,2,8,64,128]{4,3,2,1,0:T(8,128)S(1)}, u32[]{:S(2)}, u32[]{:S(2)}) collective-permute-start(f32[1,2,8,64,128]{4,3,2,1,0:T(8,128)S(1)} %collective-permute-done.2.rest_5_), channel_id=1, source_target_pairs={{0,4},{4,0},{8,12},{12,8},{16,20},{20,16},{24,28},{28,24},{1,5},{5... | collective-permute-start | bytes 1572872 | tf_op jit(solution)/shard_map/cond/branch_0_fun/ppermute | solution.py:320
  136.9 12.8 %copy-start.24 = (f32[1,2,8,64,128]{4,3,2,1,0:T(8,128)}, f32[1,2,8,64,128]{4,3,2,1,0:T(8,128)S(1)}, u32[]{:S(2)}) copy-start(f32[1,2,8,64,128]{4,3,2,1,0:T(8,128)S(1)} %collective-permute-done.3.rest_6_) | copy-start | bytes 1572868 | tf_op jit(solution)/shard_map/cond
  136.9 11.3 %collective-permute-start.7 = (f32[1,2,8,64,128]{4,3,2,1,0:T(8,128)S(1)}, f32[1,2,8,64,128]{4,3,2,1,0:T(8,128)S(1)}, u32[]{:S(2)}, u32[]{:S(2)}) collective-permute-start(f32[1,2,8,64,128]{4,3,2,1,0:T(8,128)S(1)} %collective-permute-done.3.rest_6_), channel_id=1, source_target_pairs={{0,4},{4,0},{8,12},{12,8},{16,20},{20,16},{24,28},{28,24},{1,5},{5... | collective-permute-start | bytes 1572872 | tf_op jit(solution)/shard_map/cond/branch_0_fun/ppermute | solution.py:320
  142.4 7.2 %copy-start.25 = (f32[1,2,8,64,128]{4,3,2,1,0:T(8,128)}, f32[1,2,8,64,128]{4,3,2,1,0:T(8,128)S(1)}, u32[]{:S(2)}) copy-start(f32[1,2,8,64,128]{4,3,2,1,0:T(8,128)S(1)} %collective-permute-done.4.rest_7_) | copy-start | bytes 1572868 | tf_op jit(solution)/shard_map/cond
  142.4 7.2 %collective-permute-start.8 = (f32[1,2,8,64,128]{4,3,2,1,0:T(8,128)S(1)}, f32[1,2,8,64,128]{4,3,2,1,0:T(8,128)S(1)}, u32[]{:S(2)}, u32[]{:S(2)}) collective-permute-start(f32[1,2,8,64,128]{4,3,2,1,0:T(8,128)S(1)} %collective-permute-done.4.rest_7_), channel_id=1, source_target_pairs={{0,4},{4,0},{8,12},{12,8},{16,20},{20,16},{24,28},{28,24},{1,5},{5... | collective-permute-start | bytes 1572872 | tf_op jit(solution)/shard_map/cond/branch_0_fun/ppermute | solution.py:320
  (7 other events, 10.7 us)

commit v2 on v1

--- a/solution.py
+++ b/solution.py
@@ -16,59 +16,196 @@
 
 F32 = jnp.float32
 MIB = 1 << 20
+MESH = pl.DeviceIdType.MESH
 CHUNKS = 2
 
 
-def edges_kernel(state_ref, mask_ref, lat_ref, lon_ref):
+def halo_kernel(
+    plan_ref,
+    state_ref,
+    mask_ref,
+    north_ref,
+    south_ref,
+    west_ref,
+    east_ref,
+    most_ref,
+    lat_pack,
+    lon_pack,
+    north_in,
+    south_in,
+    west_in,
+    east_in,
+    count,
+    counts_in,
+    send_sem,
+    recv_sem,
+):
     levels, rows, lanes = state_ref.shape[1:]
     half = rows // 2
     field = pl.program_id(0)
+    last_field = pl.num_programs(0) - 1
     lane = lax.broadcasted_iota(jnp.int32, (8, lanes), 1)
+    devices, bands = lax.axis_size("lon"), lax.axis_size("lat")
+    lon, lat = lax.axis_index("lon"), lax.axis_index("lat")
+    top = lat == bands - 1
+    to_east = {"lon": lax.rem(lon + 1, devices)}
+    to_west = {"lon": lax.rem(lon + devices - 1, devices)}
+    across = {"lon": devices - 1 - lon}
+    others = [{"lat": lax.rem(lat + o, bands)} for o in range(1, bands)]
+    barrier = pltpu.get_barrier_semaphore()
 
     @pl.when(field == 0)
     def _():
-        lat_ref[...] = jnp.zeros_like(lat_ref)
+        for who in [to_east, to_west, across] + others:
+            pl.semaphore_signal(barrier, inc=1, device_id=who, device_id_type=MESH)
+
+        lat_pack[...] = jnp.zeros_like(lat_pack)
+
+    unroll = 4
 
     def group(g, _):
-        part = jnp.zeros((8, lanes), F32)
-        for slot in range(2):
-            at = pl.ds(pl.multiple_of(slot * half + g * 8, 8), 8)
-            wet = mask_ref[at, :].astype(F32)
-            for k in range(levels):
-                x = state_ref[0, k, at, :] * wet
-                place = 64 * slot + 2 * k
-                part = jnp.where((lane >> 1) == (place >> 1), pltpu.roll(x, place + 1, 1), part)
-        to = pl.ds(pl.multiple_of(g * 8, 8), 8)
-        lat_ref[to, :] += pltpu.roll(part, field * (2 * levels), 1)
+        for sub in range(unroll):
+            part = jnp.zeros((8, lanes), F32)
+            for slot in range(2):
+                at = pl.ds(pl.multiple_of(slot * half + (g * unroll + sub) * 8, 8), 8)
+                wet = mask_ref[at, :].astype(F32)
+                for k in range(levels):
+                    x = state_ref[0, k, at, :] * wet
+                    place = 64 * slot + 2 * k
+                    part = jnp.where((lane >> 1) == (place >> 1), pltpu.roll(x, place + 1, 1), part)
+            to = pl.ds(pl.multiple_of((g * unroll + sub) * 8, 8), 8)
+            lat_pack[to, :] += pltpu.roll(part, field * (2 * levels), 1)
         return 0
 
-    lax.fori_loop(0, half // 8, group, 0)
-    for k in range(levels):
-        lon_ref[0, k : k + 1, :] = state_ref[0, k, 0:1, :] * mask_ref[0:1, :].astype(F32)
-        lon_ref[1, k : k + 1, :] = (
-            state_ref[0, k, rows - 1 : rows, :] * mask_ref[rows - 1 : rows, :].astype(F32)
-        )
-
-
-def edges(state, mask):
+    lax.fori_loop(0, half // (8 * unroll), group, 0)
+    at_field = pl.ds(pl.multiple_of(field * levels, levels), levels)
+    first = mask_ref[0:1, :].astype(F32)
+    final = mask_ref[rows - 1 : rows, :].astype(F32)
+    lon_pack[0, at_field, :] = jnp.concatenate([state_ref[0, k, 0:1, :] for k in range(levels)], 0) * first
+    lon_pack[1, at_field, :] = (
+        jnp.concatenate([state_ref[0, k, rows - 1 : rows, :] for k in range(levels)], 0) * final
+    )
+
+    @pl.when(field == last_field)
+    def _():
+        chips = devices // 2
+        most = jnp.int32(1)
+        for chip in range(chips):
+            for way in (1, -1):
+                number = jnp.int32(0)
+                for t in range(4):
+                    number = number + leaves(plan_ref, chips, chip, t, way).astype(jnp.int32)
+                most = jnp.maximum(most, number)
+        count[...] = jnp.full(count.shape, most, jnp.int32)
+        pl.semaphore_wait(barrier, 3 + bands - 1)
+
+        def remote(source, target, at, recv_at, who):
+            return pltpu.make_async_remote_copy(
+                src_ref=source,
+                dst_ref=target,
+                send_sem=send_sem.at[at],
+                recv_sem=recv_sem.at[recv_at],
+                device_id=who,
+                device_id_type=MESH,
+            )
+
+        up = remote(lat_pack, south_in, 0, 0, {"lat": jnp.minimum(lat + 1, bands - 1)})
+        down = remote(lat_pack, north_in, 1, 1, {"lat": jnp.maximum(lat - 1, 0)})
+        fold = remote(lat_pack, north_in, 0, 1, across)
+        east = remote(lon_pack.at[1], west_in, 2, 2, to_east)
+        west = remote(lon_pack.at[0], east_in, 3, 3, to_west)
+        tell = [remote(count, counts_in.at[o], 4 + o, 4 + o, who) for o, who in enumerate(others)]
+        pl.when(top)(fold.start)
+        pl.when(jnp.logical_not(top))(up.start)
+        pl.when(lat > 0)(down.start)
+        east.start()
+        west.start()
+        for t in tell:
+            t.start()
+
+        pl.when(lat > 0)(up.wait_recv)
+
+        @pl.when(lat > 0)
+        def _():
+            south_ref[...] = south_in[...]
+
+        @pl.when(lat == 0)
+        def _():
+            south_ref[...] = jnp.zeros_like(south_ref)
+
+        east.wait_recv()
+        west_ref[...] = west_in[...]
+        west.wait_recv()
+        east_ref[...] = east_in[...]
+        down.wait_recv()
+
+        @pl.when(top)
+        def _():
+            r = lax.broadcasted_iota(jnp.int32, (half, half), 0)
+            c = lax.broadcasted_iota(jnp.int32, (half, half), 1)
+            turn = jnp.where(r + c == half - 1, 1.0, 0.0).astype(F32)
+            mirror = jnp.dot(
+                turn, north_in[...], precision=lax.Precision.HIGHEST, preferred_element_type=F32
+            )
+            place = lax.broadcasted_iota(jnp.int32, (half, lanes), 1)
+            mirror = pltpu.roll(mirror, 65, 1)
+            north_ref[...] = jnp.where((place & 63) >= 32, -mirror, mirror)
+
+        @pl.when(jnp.logical_not(top))
+        def _():
+            north_ref[...] = north_in[...]
+
+        value = count[...]
+        for o, t in enumerate(tell):
+            t.wait_recv()
+            value = jnp.maximum(value, counts_in[o])
+        most_ref[...] = value
+        up.wait_send()
+        pl.when(lat > 0)(down.wait_send)
+        east.wait_send()
+        west.wait_send()
+        for t in tell:
+            t.wait_send()
+
+
+def halos(plan, state, mask):
     fields, levels, rows, lanes = state.shape
+    bands = lax.axis_size("lat")
+    pack = (rows // 2, lanes)
+    edge = (fields * levels, lanes)
+    spec = lambda shape: pl.BlockSpec(shape, lambda f: (0, 0))
     return pl.pallas_call(
-        edges_kernel,
+        halo_kernel,
         grid=(fields,),
         in_specs=[
+            pl.BlockSpec(memory_space=pltpu.SMEM),
             pl.BlockSpec((1, levels, rows, lanes), lambda f: (f, 0, 0, 0)),
-            pl.BlockSpec((rows, lanes), lambda f: (0, 0)),
+            spec((rows, lanes)),
         ],
-        out_specs=[
-            pl.BlockSpec((rows // 2, lanes), lambda f: (0, 0)),
-            pl.BlockSpec((2, levels, lanes), lambda f: (0, f, 0)),
+        out_specs=[spec(pack), spec(pack), spec(edge), spec(edge), spec((8, lanes))],
+        out_shape=[
+            jax.ShapeDtypeStruct(pack, F32),
+            jax.ShapeDtypeStruct(pack, F32),
+            jax.ShapeDtypeStruct(edge, F32),
+            jax.ShapeDtypeStruct(edge, F32),
+            jax.ShapeDtypeStruct((8, lanes), jnp.int32),
         ],
-        out_shape=[
-            jax.ShapeDtypeStruct((rows // 2, lanes), F32),
-            jax.ShapeDtypeStruct((2, fields * levels, lanes), F32),
+        scratch_shapes=[
+            pltpu.VMEM(pack, F32),
+            pltpu.VMEM((2,) + edge, F32),
+            pltpu.VMEM(pack, F32),
+            pltpu.VMEM(pack, F32),
+            pltpu.VMEM(edge, F32),
+            pltpu.VMEM(edge, F32),
+            pltpu.VMEM((8, lanes), jnp.int32),
+            pltpu.VMEM((bands - 1, 8, lanes), jnp.int32),
+            pltpu.SemaphoreType.DMA((4 + bands - 1,)),
+            pltpu.SemaphoreType.DMA((4 + bands - 1,)),
         ],
-        compiler_params=pltpu.CompilerParams(vmem_limit_bytes=24 * MIB),
-    )(state, mask)
+        compiler_params=pltpu.CompilerParams(
+            collective_id=0, has_side_effects=True, vmem_limit_bytes=24 * MIB
+        ),
+    )(plan, state, mask)
 
 
 def step_kernel(
@@ -213,7 +350,7 @@
 
 
 def pack_kernel(rounds, chips, plan_ref, mine, other, *rest):
-    outs, sem = rest[:-1], rest[-1]
+    outs, held, sem, out_sem = rest[:-3], rest[-3], rest[-2], rest[-1]
     chip, core = chip_of()
     fields = mine.shape[1]
     span = fields // CHUNKS
@@ -235,22 +372,27 @@
             slot = lax.rem(chosen, 2)
             for is_own, source in ((True, mine), (False, other)):
                 copy = pltpu.make_async_copy(
-                    source.at[slot, pl.ds(chunk * span, span)], out.at[r], sem.at[at]
+                    source.at[slot, pl.ds(chunk * span, span)], held.at[at], sem.at[at]
                 )
                 pl.when(own if is_own else jnp.logical_not(own))(copy.start)
             at += 1
     at = 0
+    writes = []
     for chunk in range(CHUNKS):
         for way, r, chosen in jobs:
             out = outs[chunk * 2 + (0 if way == 1 else 1)]
-            pltpu.make_async_copy(mine.at[0, pl.ds(chunk * span, span)], out.at[r], sem.at[at]).wait()
+            pltpu.make_async_copy(mine.at[0, pl.ds(chunk * span, span)], held.at[at], sem.at[at]).wait()
+            writes.append(pltpu.make_async_copy(held.at[at], out.at[r], out_sem.at[at]))
+            writes[-1].start()
             at += 1
+    for write in writes:
+        write.wait()
 
 
 def place_kernel(rounds, chips, plan_ref, *rest):
     mine, theirs, other, other_theirs = rest[:4]
-    arrived = rest[4:-2]
-    out, sem = rest[-2:]
+    arrived = rest[4:-4]
+    out, kept, sem, out_sem = rest[-4:]
     chip, core = chip_of()
     fields, quarter = mine.shape[1], mine.shape[3]
     span = fields // CHUNKS
@@ -272,8 +414,9 @@
             row = pl.multiple_of(2 * quarter * slot + half * quarter, quarter)
             for chunk in range(CHUNKS):
                 where_f = pl.ds(chunk * span, span)
-                to = out.at[where_f, :, pl.ds(row, quarter), :]
-                s = sem.at[(slot * 2 + part) * CHUNKS + chunk]
+                job = (slot * 2 + part) * CHUNKS + chunk
+                to = kept.at[job]
+                s = sem.at[job]
                 held = mine if part == 0 else theirs
                 held_other = other if part == 0 else other_theirs
                 pl.when(local & own)(
@@ -291,9 +434,14 @@
                     rank = jnp.minimum(rank, rounds - 1)
                     buffer = arrived[(part * CHUNKS + chunk) * 2 + side]
                     pl.when(came)(pltpu.make_async_copy(buffer.at[rank], to, s).start)
-                waits.append((held.at[0, where_f], to, s))
-    for a, b, s in waits:
+                waits.append((held.at[0, where_f], to, s, out.at[where_f, :, pl.ds(row, quarter), :], out_sem.at[job]))
+    writes = []
+    for a, b, s, to, out_s in waits:
         pltpu.make_async_copy(a, b, s).wait()
+        writes.append(pltpu.make_async_copy(b, to, out_s))
+        writes[-1].start()
+    for write in writes:
+        write.wait()
 
 
 def exchange(rounds, plan, mine, theirs, other):
@@ -310,7 +458,12 @@
         in_specs=[scalars, anywhere, anywhere],
         out_specs=[anywhere] * (2 * CHUNKS),
         out_shape=[piece] * (2 * CHUNKS),
-        scratch_shapes=[pltpu.SemaphoreType.DMA((2 * CHUNKS * rounds,))],
+        scratch_shapes=[
+            pltpu.VMEM((2 * CHUNKS * rounds, span, levels, quarter, lanes), F32),
+            pltpu.SemaphoreType.DMA((2 * CHUNKS * rounds,)),
+            pltpu.SemaphoreType.DMA((2 * CHUNKS * rounds,)),
+        ],
+        compiler_params=pltpu.CompilerParams(vmem_limit_bytes=24 * MIB),
     )(plan, mine, other)
     arrived = []
     for at, send in enumerate(sends):
@@ -323,47 +476,23 @@
         in_specs=[scalars] + [anywhere] * (4 + 4 * CHUNKS),
         out_specs=anywhere,
         out_shape=jax.ShapeDtypeStruct((fields, levels, 4 * quarter, lanes), F32),
-        scratch_shapes=[pltpu.SemaphoreType.DMA((4 * CHUNKS,))],
+        scratch_shapes=[
+            pltpu.VMEM((4 * CHUNKS, span, levels, quarter, lanes), F32),
+            pltpu.SemaphoreType.DMA((4 * CHUNKS,)),
+            pltpu.SemaphoreType.DMA((4 * CHUNKS,)),
+        ],
+        compiler_params=pltpu.CompilerParams(vmem_limit_bytes=24 * MIB),
     )(plan, mine, theirs, other, other_theirs, *arrived, *swapped)
 
 
-def most_rounds(plan, chips):
-    target = (plan // 4).reshape(chips, 4)
-    home = jnp.arange(chips, dtype=jnp.int32)[:, None]
-    apart = jnp.mod(target - home, chips)
-    east = jnp.max(jnp.sum((apart == 1).astype(jnp.int32), axis=1))
-    west = jnp.max(jnp.sum((apart == chips - 1).astype(jnp.int32), axis=1))
-    most = jnp.maximum(east, west)
-    rows = lax.axis_size("lat")
-    apart = 1
-    while apart < rows:
-        most = jnp.maximum(most, lax.ppermute(most, "lat", [(i, i ^ apart) for i in range(rows)]))
-        apart *= 2
-    return most
-
-
 def local(state, diffusivity, mask, tile_plan):
-    devices, bands = lax.axis_size("lon"), lax.axis_size("lat")
+    devices = lax.axis_size("lon")
     plan = tile_plan.reshape(-1)
-    most = most_rounds(plan, devices // 2)
-    lat_pack, lon_pack = edges(state, mask)
-    fold = lax.ppermute(
-        lat_pack,
-        ("lon", "lat"),
-        [(i * bands + bands - 1, (devices - 1 - i) * bands + bands - 1) for i in range(devices)],
-    )
-    above = lax.ppermute(lat_pack, "lat", [(i + 1, i) for i in range(bands - 1)])
-    south = lax.ppermute(lat_pack, "lat", [(i, i + 1) for i in range(bands - 1)])
-    west = lax.ppermute(lon_pack[1], "lon", [(i, (i + 1) % devices) for i in range(devices)])
-    east = lax.ppermute(lon_pack[0], "lon", [((i + 1) % devices, i) for i in range(devices)])
-    lanes = state.shape[3]
-    sign = jnp.where(jnp.arange(lanes) % 64 >= 32, -1.0, 1.0).astype(F32)
-    mirror = jnp.roll(fold[::-1], 65, axis=1) * sign
-    north = jnp.where(lax.axis_index("lat") == bands - 1, mirror, above)
+    north, south, west, east, most = halos(plan, state, mask)
     theirs, mine = step(state, diffusivity, mask, north, south, west, east)
     other = lax.ppermute(theirs, "lon", [(i, i ^ 1) for i in range(devices)])
     branches = [functools.partial(exchange, rounds) for rounds in (1, 2, 3)]
-    return lax.switch(jnp.clip(most - 1, 0, 2), branches, plan, mine, theirs, other)
+    return lax.switch(jnp.clip(most[0, 0] - 1, 0, 2), branches, plan, mine, theirs, other)
 
 
 def solution(mesh):

time: 280 us -> 86.2 us (0.31)
  Pallas kernels: 152 us -> 22.9 us
  starting transfers between devices: 108 us -> 12.2 us
  waiting for transfers between devices: 7.4 us -> 42.9 us
    pallas_call x1, Pallas kernels: 129 us -> 1.48 us  [exchange(): pl.pallas_call(functools.partial(place_kernel, rounds, chips), in_specs=[...]
    ppermute x4, starting transfers between devices: 81.3 us -> 5.48 us  [exchange(): swapped = [lax.ppermute(a, 'lon', swap) for a in arrived]]
    ppermute x4, waiting for transfers between devices: 4.42 us -> 38.8 us  [exchange(): lax.ppermute(send, 'lon', [(i, (i + by) % devices) for i in range(devices)])]
    ppermute x7 -> x0, starting transfers between devices: 16.7 us -> none  [the longest x2 8.53 us: most_rounds(): lax.ppermute(most, 'lat', [(i, i ^ apart) for i in range(rows)])]
    unnamed x13 -> x14, local copies, waits for them, and re-layouts: 5.8 us -> 6.28 us
  transfers between devices with their start and end apart: 17 -> 10, of which waited for: 6 -> 6; matrix products, arithmetic and copies ran while one was open for 1% -> 1% of each run, Pallas kernels for 1% -> 1%
where the time goes in v2:
time: 86.2 us; the launch traced here: 85.7 us
  waiting for transfers between devices  42.9 us (50%)
  Pallas kernels  22.9 us (27%)
  starting transfers between devices  12.2 us (14%)
  local copies, waits for them, and re-layouts  6.8 us (8%)
    ppermute x4, waiting for transfers between devices, exchange(): lax.ppermute(send, 'lon', [(i, (i + by) % devices) for i in range(devices)])  38.8 us
    pallas_call x1, Pallas kernels, halos(): pl.pallas_call(halo_kernel, grid=(fields,), in_specs=[pl.BlockSpec(memory...  10.3 us
    pallas_call x1, Pallas kernels, step(): pl.pallas_call(step_kernel, grid=(4,), in_specs=[whole(a) for a in (state...  10.2 us
    unnamed x14, local copies, waits for them, and re-layouts  6.28 us
    ppermute x4, starting transfers between devices, exchange(): swapped = [lax.ppermute(a, 'lon', swap) for a in arrived]  5.48 us
    ppermute x4, starting transfers between devices, exchange(): lax.ppermute(send, 'lon', [(i, (i + by) % devices) for i in range(devices)])  4.78 us
    ppermute x1, waiting for transfers between devices, local(): other = lax.ppermute(theirs, 'lon', [(i, i ^ 1) for i in range(devices)])  2.62 us
  transfers between devices with their start and end apart: 10, of which 6 were waited for; matrix products, arithmetic and copies ran while one was open for 1% of the time, Pallas kernels for 1%

profile of v2, /device:TPU:1, one launch (start us, length us, event | category | flops | bytes accessed | tf_op | source)
XLA Modules:
  0.0 85.7 jit_solution(16729730008056018150)
XLA Ops:
  0.0 2.2 %copy-done = f32[4,8,256,128]{3,2,1,0:T(8,128)S(1)} copy-done((f32[4,8,256,128]{3,2,1,0:T(8,128)S(1)}, f32[4,8,256,128]{3,2,1,0:T(8,128)}, u32[]{:S(2)}) %copy-start) | copy-done | bytes 4194328
  2.2 0.9 %copy-done.3 = s32[256,128]{1,0:T(8,128)S(1)} copy-done((s32[256,128]{1,0:T(8,128)S(1)}, s32[256,128]{1,0:T(8,128)}, u32[]{:S(2)}) %copy-start.3) | copy-done | bytes 131096
  3.1 10.3 %shard_map.49 = (f32[128,128]{1,0:T(8,128)S(1)}, f32[128,128]{1,0:T(8,128)S(1)}, f32[32,128]{1,0:T(8,128)S(1)}, f32[32,128]{1,0:T(8,128)S(1)}, s32[8,128]{1,0:T(8,128)S(1)}) custom-call(s32[16]{0:T(128)} %bitcast.2, f32[4,8,256,128]{3,2,1,0:T(8,128)S(1)} %copy-done, s32[256,128]{1,0:T(8,128)S(1)} %copy-done.3), custom_call_target="tpu_custom_call" | custom-call | tf_op jit(solution)/shard_map/pallas_call | solution.py:177
  13.4 1.2 %copy-done.2 = f32[7,256,128]{2,1,0:T(8,128)S(1)} copy-done((f32[7,256,128]{2,1,0:T(8,128)S(1)}, f32[7,256,128]{2,1,0:T(8,128)}, u32[]{:S(2)}) %copy-start.2) | copy-done | bytes 917528
  14.6 10.2 %shard_map.50 = (f32[2,4,8,64,128]{4,3,2,1,0:T(8,128)S(1)}, f32[2,4,8,64,128]{4,3,2,1,0:T(8,128)S(1)}) custom-call(f32[4,8,256,128]{3,2,1,0:T(8,128)S(1)} %copy-done.1, f32[7,256,128]{2,1,0:T(8,128)S(1)} %copy-done.2, s32[256,128]{1,0:T(8,128)S(1)} %copy-done.4, f32[128,128]{1,0:T(8,128)S(1)} %get-tuple-element.65.north_ref, ...), custom_call_target="tpu_custom_call" | custom-call | tf_op jit(solution)/shard_map/pallas_call | solution.py:329
  24.8 1.6 %collective-permute-start.27 = (f32[2,4,8,64,128]{4,3,2,1,0:T(8,128)S(1)}, f32[2,4,8,64,128]{4,3,2,1,0:T(8,128)S(1)}, u32[]{:S(2)}, u32[]{:S(2)}) collective-permute-start(f32[2,4,8,64,128]{4,3,2,1,0:T(8,128)S(1)} %get-tuple-element.70), channel_id=1, source_target_pairs={{0,4},{4,0},{8,12},{12,8},{16,20},{20,16},{24,28},{28,24},{1,5},{5... | collective-permute-start | bytes 6291464 | tf_op jit(solution)/shard_map/ppermute | solution.py:493
  26.4 0.5 slice.3
  27.6 2.6 %collective-permute-done.27 = f32[2,4,8,64,128]{4,3,2,1,0:T(8,128)S(1)} collective-permute-done((f32[2,4,8,64,128]{4,3,2,1,0:T(8,128)S(1)}, f32[2,4,8,64,128]{4,3,2,1,0:T(8,128)S(1)}, u32[]{:S(2)}, u32[]{:S(2)}) %collective-permute-start.27) | collective-permute-done | bytes 2097184 | tf_op jit(solution)/shard_map/ppermute | solution.py:493
  30.2 53.5 %conditional.1 = (f32[4,8,256,128]{3,2,1,0:T(8,128)S(1)}) conditional(s32[]{:T(128)} %bitcast.1, (f32[2,4,8,64,128]{4,3,2,1,0:T(8,128)S(1)}, s32[16]{0:T(128)S(1)}, f32[2,4,8,64,128]{4,3,2,1,0:T(8,128)S(1)}, f32[2,4,8,64,128]{4,3,2,1,0:T(8,128)S(1)}) %tuple.22, (f32[2,4,8,64,128]{4,3,2,1,0:T(8,128)S(1)}, s32[16]{0:T(128)S(1)}, ...), branch_computations={%region_0.1_spmd, %region_1.2_spmd, %region_2.3_spmd} | conditional | bytes 58720624 | solution.py:495
  30.5 1.0 %branch_0_fun.2 = (f32[1,2,8,64,128]{4,3,2,1,0:T(8,128)S(1)}, f32[1,2,8,64,128]{4,3,2,1,0:T(8,128)S(1)}, f32[1,2,8,64,128]{4,3,2,1,0:T(8,128)S(1)}, f32[1,2,8,64,128]{4,3,2,1,0:T(8,128)S(1)}) custom-call(s32[16]{0:T(128)S(1)} %get-tuple-element.32.plan_ref, f32[2,4,8,64,128]{4,3,2,1,0:T(8,128)S(1)} %get-tuple-element.34.mine.rest_0_, ...), custom_call_target="tpu_custom_call" | custom-call | tf_op jit(solution)/shard_map/cond/branch_0_fun/pallas_call | solution.py:456
  31.5 1.3 %collective-permute-start.1 = (f32[1,2,8,64,128]{4,3,2,1,0:T(8,128)S(1)}, f32[1,2,8,64,128]{4,3,2,1,0:T(8,128)S(1)}, u32[]{:S(2)}, u32[]{:S(2)}) collective-permute-start(f32[1,2,8,64,128]{4,3,2,1,0:T(8,128)S(1)} %get-tuple-element.37), channel_id=1, source_target_pairs={{0,8},{4,12},{8,16},{12,20},{16,24},{20,28},{24,0},{28,4},{1,9},{5... | collective-permute-start | bytes 1572872 | tf_op jit(solution)/shard_map/cond/branch_0_fun/ppermute | solution.py:471
  32.8 1.2 %collective-permute-start.2 = (f32[1,2,8,64,128]{4,3,2,1,0:T(8,128)S(1)}, f32[1,2,8,64,128]{4,3,2,1,0:T(8,128)S(1)}, u32[]{:S(2)}, u32[]{:S(2)}) collective-permute-start(f32[1,2,8,64,128]{4,3,2,1,0:T(8,128)S(1)} %get-tuple-element.38), channel_id=1, source_target_pairs={{0,24},{4,28},{8,0},{12,4},{16,8},{20,12},{24,16},{28,20},{1,25},{... | collective-permute-start | bytes 1572872 | tf_op jit(solution)/shard_map/cond/branch_0_fun/ppermute | solution.py:471
  34.3 2.1 %collective-permute-start.4 = (f32[1,2,8,64,128]{4,3,2,1,0:T(8,128)S(1)}, f32[1,2,8,64,128]{4,3,2,1,0:T(8,128)S(1)}, u32[]{:S(2)}, u32[]{:S(2)}) collective-permute-start(f32[1,2,8,64,128]{4,3,2,1,0:T(8,128)S(1)} %get-tuple-element.40), channel_id=1, source_target_pairs={{0,24},{4,28},{8,0},{12,4},{16,8},{20,12},{24,16},{28,20},{1,25},{... | collective-permute-start | bytes 1572872 | tf_op jit(solution)/shard_map/cond/branch_0_fun/ppermute | solution.py:471
  36.3 9.6 %collective-permute-done.1.rest_4_ = f32[1,2,8,64,128]{4,3,2,1,0:T(8,128)S(1)} collective-permute-done((f32[1,2,8,64,128]{4,3,2,1,0:T(8,128)S(1)}, f32[1,2,8,64,128]{4,3,2,1,0:T(8,128)S(1)}, u32[]{:S(2)}, u32[]{:S(2)}) %collective-permute-start.1) | collective-permute-done | bytes 524320 | tf_op jit(solution)/shard_map/cond/branch_0_fun/ppermute | solution.py:471
  45.9 1.5 %collective-permute-start.5 = (f32[1,2,8,64,128]{4,3,2,1,0:T(8,128)S(1)}, f32[1,2,8,64,128]{4,3,2,1,0:T(8,128)S(1)}, u32[]{:S(2)}, u32[]{:S(2)}) collective-permute-start(f32[1,2,8,64,128]{4,3,2,1,0:T(8,128)S(1)} %collective-permute-done.1.rest_4_), channel_id=1, source_target_pairs={{0,4},{4,0},{8,12},{12,8},{16,20},{20,16},{24,28},{28,24},{1,5},{5... | collective-permute-start | bytes 1572872 | tf_op jit(solution)/shard_map/cond/branch_0_fun/ppermute | solution.py:473
  47.4 9.8 %collective-permute-done.2.rest_5_ = f32[1,2,8,64,128]{4,3,2,1,0:T(8,128)S(1)} collective-permute-done((f32[1,2,8,64,128]{4,3,2,1,0:T(8,128)S(1)}, f32[1,2,8,64,128]{4,3,2,1,0:T(8,128)S(1)}, u32[]{:S(2)}, u32[]{:S(2)}) %collective-permute-start.2) | collective-permute-done | bytes 524320 | tf_op jit(solution)/shard_map/cond/branch_0_fun/ppermute | solution.py:471
  57.2 1.5 %collective-permute-start.6 = (f32[1,2,8,64,128]{4,3,2,1,0:T(8,128)S(1)}, f32[1,2,8,64,128]{4,3,2,1,0:T(8,128)S(1)}, u32[]{:S(2)}, u32[]{:S(2)}) collective-permute-start(f32[1,2,8,64,128]{4,3,2,1,0:T(8,128)S(1)} %collective-permute-done.2.rest_5_), channel_id=1, source_target_pairs={{0,4},{4,0},{8,12},{12,8},{16,20},{20,16},{24,28},{28,24},{1,5},{5... | collective-permute-start | bytes 1572872 | tf_op jit(solution)/shard_map/cond/branch_0_fun/ppermute | solution.py:473
  58.7 9.7 %collective-permute-done.3.rest_6_ = f32[1,2,8,64,128]{4,3,2,1,0:T(8,128)S(1)} collective-permute-done((f32[1,2,8,64,128]{4,3,2,1,0:T(8,128)S(1)}, f32[1,2,8,64,128]{4,3,2,1,0:T(8,128)S(1)}, u32[]{:S(2)}, u32[]{:S(2)}) %collective-permute-start.3) | collective-permute-done | bytes 524320 | tf_op jit(solution)/shard_map/cond/branch_0_fun/ppermute | solution.py:471
  68.4 1.5 %collective-permute-start.7 = (f32[1,2,8,64,128]{4,3,2,1,0:T(8,128)S(1)}, f32[1,2,8,64,128]{4,3,2,1,0:T(8,128)S(1)}, u32[]{:S(2)}, u32[]{:S(2)}) collective-permute-start(f32[1,2,8,64,128]{4,3,2,1,0:T(8,128)S(1)} %collective-permute-done.3.rest_6_), channel_id=1, source_target_pairs={{0,4},{4,0},{8,12},{12,8},{16,20},{20,16},{24,28},{28,24},{1,5},{5... | collective-permute-start | bytes 1572872 | tf_op jit(solution)/shard_map/cond/branch_0_fun/ppermute | solution.py:473
  69.9 9.8 %collective-permute-done.4.rest_7_ = f32[1,2,8,64,128]{4,3,2,1,0:T(8,128)S(1)} collective-permute-done((f32[1,2,8,64,128]{4,3,2,1,0:T(8,128)S(1)}, f32[1,2,8,64,128]{4,3,2,1,0:T(8,128)S(1)}, u32[]{:S(2)}, u32[]{:S(2)}) %collective-permute-start.4) | collective-permute-done | bytes 524320 | tf_op jit(solution)/shard_map/cond/branch_0_fun/ppermute | solution.py:471
  79.6 1.0 %collective-permute-start.8 = (f32[1,2,8,64,128]{4,3,2,1,0:T(8,128)S(1)}, f32[1,2,8,64,128]{4,3,2,1,0:T(8,128)S(1)}, u32[]{:S(2)}, u32[]{:S(2)}) collective-permute-start(f32[1,2,8,64,128]{4,3,2,1,0:T(8,128)S(1)} %collective-permute-done.4.rest_7_), channel_id=1, source_target_pairs={{0,4},{4,0},{8,12},{12,8},{16,20},{20,16},{24,28},{28,24},{1,5},{5... | collective-permute-start | bytes 1572872 | tf_op jit(solution)/shard_map/cond/branch_0_fun/ppermute | solution.py:473
  80.6 1.5 %collective-permute-done.8.rest_11_ = f32[1,2,8,64,128]{4,3,2,1,0:T(8,128)S(1)} collective-permute-done((f32[1,2,8,64,128]{4,3,2,1,0:T(8,128)S(1)}, f32[1,2,8,64,128]{4,3,2,1,0:T(8,128)S(1)}, u32[]{:S(2)}, u32[]{:S(2)}) %collective-permute-start.8) | collective-permute-done | bytes 524320 | tf_op jit(solution)/shard_map/cond/branch_0_fun/ppermute | solution.py:473
  82.1 1.5 %branch_0_fun.3 = f32[4,8,256,128]{3,2,1,0:T(8,128)S(1)} custom-call(s32[16]{0:T(128)S(1)} %get-tuple-element.32.plan_ref, f32[2,4,8,64,128]{4,3,2,1,0:T(8,128)S(1)} %get-tuple-element.34.mine.rest_0_, f32[2,4,8,64,128]{4,3,2,1,0:T(8,128)S(1)} %get-tuple-element.35.rest_1_, f32[2,4,8,64,128]{4,3,2,1,0:T(8,128)S(1)} %get-tuple-element.36.other.rest_2_, ...), custom_call_target="tpu_custom_call" | custom-call | tf_op jit(solution)/shard_map/cond/branch_0_fun/pallas_call | solution.py:474
  83.7 2.0 %copy-done.5 = f32[4,8,256,128]{3,2,1,0:T(8,128)} copy-done((f32[4,8,256,128]{3,2,1,0:T(8,128)}, f32[4,8,256,128]{3,2,1,0:T(8,128)S(1)}, u32[]{:S(2)}) %copy-start.5) | copy-done | bytes 4194328
  (16 shorter events, 0.7 us)
Async XLA Ops:
  0.0 2.2 %copy-start = (f32[4,8,256,128]{3,2,1,0:T(8,128)S(1)}, f32[4,8,256,128]{3,2,1,0:T(8,128)}, u32[]{:S(2)}) copy-start(f32[4,8,256,128]{3,2,1,0:T(8,128)} %state_ref.3) | copy-start | bytes 12582916
  2.2 0.9 %copy-start.3 = (s32[256,128]{1,0:T(8,128)S(1)}, s32[256,128]{1,0:T(8,128)}, u32[]{:S(2)}) copy-start(s32[256,128]{1,0:T(8,128)} %mask_ref.3) | copy-start | bytes 393220
  3.1 10.3 %copy-start.1 = (f32[4,8,256,128]{3,2,1,0:T(8,128)S(1)}, f32[4,8,256,128]{3,2,1,0:T(8,128)}, u32[]{:S(2)}) copy-start(f32[4,8,256,128]{3,2,1,0:T(8,128)} %state_ref.3) | copy-start | bytes 12582916
  3.1 10.3 %copy-start.4 = (s32[256,128]{1,0:T(8,128)S(1)}, s32[256,128]{1,0:T(8,128)}, u32[]{:S(2)}) copy-start(s32[256,128]{1,0:T(8,128)} %mask_ref.3) | copy-start | bytes 393220
  13.4 1.2 %copy-start.2 = (f32[7,256,128]{2,1,0:T(8,128)S(1)}, f32[7,256,128]{2,1,0:T(8,128)}, u32[]{:S(2)}) copy-start(f32[7,256,128]{2,1,0:T(8,128)} %diff_ref.1) | copy-start | bytes 2752516
  14.6 15.6 %copy-start.6 = (s32[16,1]{0,1:T(1,128)S(1)}, s32[16,1]{0,1:T(1,128)}, u32[]{:S(2)}) copy-start(s32[16,1]{0,1:T(1,128)} %param.10) | copy-start | bytes 196
  24.8 5.4 %collective-permute-start.27 = (f32[2,4,8,64,128]{4,3,2,1,0:T(8,128)S(1)}, f32[2,4,8,64,128]{4,3,2,1,0:T(8,128)S(1)}, u32[]{:S(2)}, u32[]{:S(2)}) collective-permute-start(f32[2,4,8,64,128]{4,3,2,1,0:T(8,128)S(1)} %get-tuple-element.70), channel_id=1, source_target_pairs={{0,4},{4,0},{8,12},{12,8},{16,20},{20,16},{24,28},{28,24},{1,5},{5... | collective-permute-start | bytes 6291464 | tf_op jit(solution)/shard_map/ppermute | solution.py:493
  30.2 52.0 %collective-permute-start = (f32[2,4,8,64,128]{4,3,2,1,0:T(8,128)S(1)}, f32[2,4,8,64,128]{4,3,2,1,0:T(8,128)S(1)}, u32[]{:S(2)}, u32[]{:S(2)}) collective-permute-start(f32[2,4,8,64,128]{4,3,2,1,0:T(8,128)S(1)} %get-tuple-element.34.mine.rest_0_), channel_id=1, source_target_pairs={{0,4},{4,0},{8,12},{12,8},{16,20},{20,16},{24,28},{28,24},{1,5},{5... | collective-permute-start | bytes 6291464 | tf_op jit(solution)/shard_map/cond/branch_0_fun/ppermute | solution.py:472
  31.5 14.3 %collective-permute-start.1 = (f32[1,2,8,64,128]{4,3,2,1,0:T(8,128)S(1)}, f32[1,2,8,64,128]{4,3,2,1,0:T(8,128)S(1)}, u32[]{:S(2)}, u32[]{:S(2)}) collective-permute-start(f32[1,2,8,64,128]{4,3,2,1,0:T(8,128)S(1)} %get-tuple-element.37), channel_id=1, source_target_pairs={{0,8},{4,12},{8,16},{12,20},{16,24},{20,28},{24,0},{28,4},{1,9},{5... | collective-permute-start | bytes 1572872 | tf_op jit(solution)/shard_map/cond/branch_0_fun/ppermute | solution.py:471
  32.8 24.4 %collective-permute-start.2 = (f32[1,2,8,64,128]{4,3,2,1,0:T(8,128)S(1)}, f32[1,2,8,64,128]{4,3,2,1,0:T(8,128)S(1)}, u32[]{:S(2)}, u32[]{:S(2)}) collective-permute-start(f32[1,2,8,64,128]{4,3,2,1,0:T(8,128)S(1)} %get-tuple-element.38), channel_id=1, source_target_pairs={{0,24},{4,28},{8,0},{12,4},{16,8},{20,12},{24,16},{28,20},{1,25},{... | collective-permute-start | bytes 1572872 | tf_op jit(solution)/shard_map/cond/branch_0_fun/ppermute | solution.py:471
  34.0 34.4 %collective-permute-start.3 = (f32[1,2,8,64,128]{4,3,2,1,0:T(8,128)S(1)}, f32[1,2,8,64,128]{4,3,2,1,0:T(8,128)S(1)}, u32[]{:S(2)}, u32[]{:S(2)}) collective-permute-start(f32[1,2,8,64,128]{4,3,2,1,0:T(8,128)S(1)} %get-tuple-element.39), channel_id=1, source_target_pairs={{0,8},{4,12},{8,16},{12,20},{16,24},{20,28},{24,0},{28,4},{1,9},{5... | collective-permute-start | bytes 1572872 | tf_op jit(solution)/shard_map/cond/branch_0_fun/ppermute | solution.py:471
  34.3 45.4 %collective-permute-start.4 = (f32[1,2,8,64,128]{4,3,2,1,0:T(8,128)S(1)}, f32[1,2,8,64,128]{4,3,2,1,0:T(8,128)S(1)}, u32[]{:S(2)}, u32[]{:S(2)}) collective-permute-start(f32[1,2,8,64,128]{4,3,2,1,0:T(8,128)S(1)} %get-tuple-element.40), channel_id=1, source_target_pairs={{0,24},{4,28},{8,0},{12,4},{16,8},{20,12},{24,16},{28,20},{1,25},{... | collective-permute-start | bytes 1572872 | tf_op jit(solution)/shard_map/cond/branch_0_fun/ppermute | solution.py:471
  45.9 34.7 %collective-permute-start.5 = (f32[1,2,8,64,128]{4,3,2,1,0:T(8,128)S(1)}, f32[1,2,8,64,128]{4,3,2,1,0:T(8,128)S(1)}, u32[]{:S(2)}, u32[]{:S(2)}) collective-permute-start(f32[1,2,8,64,128]{4,3,2,1,0:T(8,128)S(1)} %collective-permute-done.1.rest_4_), channel_id=1, source_target_pairs={{0,4},{4,0},{8,12},{12,8},{16,20},{20,16},{24,28},{28,24},{1,5},{5... | collective-permute-start | bytes 1572872 | tf_op jit(solution)/shard_map/cond/branch_0_fun/ppermute | solution.py:473
  57.2 23.4 %collective-permute-start.6 = (f32[1,2,8,64,128]{4,3,2,1,0:T(8,128)S(1)}, f32[1,2,8,64,128]{4,3,2,1,0:T(8,128)S(1)}, u32[]{:S(2)}, u32[]{:S(2)}) collective-permute-start(f32[1,2,8,64,128]{4,3,2,1,0:T(8,128)S(1)} %collective-permute-done.2.rest_5_), channel_id=1, source_target_pairs={{0,4},{4,0},{8,12},{12,8},{16,20},{20,16},{24,28},{28,24},{1,5},{5... | collective-permute-start | bytes 1572872 | tf_op jit(solution)/shard_map/cond/branch_0_fun/ppermute | solution.py:473
  68.4 12.3 %collective-permute-start.7 = (f32[1,2,8,64,128]{4,3,2,1,0:T(8,128)S(1)}, f32[1,2,8,64,128]{4,3,2,1,0:T(8,128)S(1)}, u32[]{:S(2)}, u32[]{:S(2)}) collective-permute-start(f32[1,2,8,64,128]{4,3,2,1,0:T(8,128)S(1)} %collective-permute-done.3.rest_6_), channel_id=1, source_target_pairs={{0,4},{4,0},{8,12},{12,8},{16,20},{20,16},{24,28},{28,24},{1,5},{5... | collective-permute-start | bytes 1572872 | tf_op jit(solution)/shard_map/cond/branch_0_fun/ppermute | solution.py:473
  79.6 2.5 %collective-permute-start.8 = (f32[1,2,8,64,128]{4,3,2,1,0:T(8,128)S(1)}, f32[1,2,8,64,128]{4,3,2,1,0:T(8,128)S(1)}, u32[]{:S(2)}, u32[]{:S(2)}) collective-permute-start(f32[1,2,8,64,128]{4,3,2,1,0:T(8,128)S(1)} %collective-permute-done.4.rest_7_), channel_id=1, source_target_pairs={{0,4},{4,0},{8,12},{12,8},{16,20},{20,16},{24,28},{28,24},{1,5},{5... | collective-permute-start | bytes 1572872 | tf_op jit(solution)/shard_map/cond/branch_0_fun/ppermute | solution.py:473
  83.6 2.0 %copy-start.5 = (f32[4,8,256,128]{3,2,1,0:T(8,128)}, f32[4,8,256,128]{3,2,1,0:T(8,128)S(1)}, u32[]{:S(2)}) copy-start(f32[4,8,256,128]{3,2,1,0:T(8,128)S(1)} %get-tuple-element.131) | copy-start | bytes 12582916

commit v3 on v2

v3 whole, which is shorter than its diff:
```python
import functools

import jax
import jax.numpy as jnp
from jax import lax
from jax.experimental import pallas as pl
from jax.experimental.pallas import tpu as pltpu
from jax.sharding import PartitionSpec as P

advect_coef = 0.1
diffuse_coef = 0.1
gradient_coef = 0.1
thermal_coef = 0.2
haline_coef = 0.15
weight_coef = 0.25

F32 = jnp.float32
MIB = 1 << 20
MESH = pl.DeviceIdType.MESH
CHUNKS = 2


def halo_kernel(
    plan_ref,
    state_ref,
    mask_ref,
    north_ref,
    south_ref,
    west_ref,
    east_ref,
    most_ref,
    lat_pack,
    lon_pack,
    north_in,
    south_in,
    west_in,
    east_in,
    count,
    counts_in,
    send_sem,
    recv_sem,
):
    levels, rows, lanes = state_ref.shape[1:]
    half = rows // 2
    field = pl.program_id(0)
    last_field = pl.num_programs(0) - 1
    lane = lax.broadcasted_iota(jnp.int32, (8, lanes), 1)
    devices, bands = lax.axis_size("lon"), lax.axis_size("lat")
    lon, lat = lax.axis_index("lon"), lax.axis_index("lat")
    top = lat == bands - 1
    to_east = {"lon": lax.rem(lon + 1, devices)}
    to_west = {"lon": lax.rem(lon + devices - 1, devices)}
    across = {"lon": devices - 1 - lon}
    others = [{"lat": lax.rem(lat + o, bands)} for o in range(1, bands)]
    barrier = pltpu.get_barrier_semaphore()

    @pl.when(field == 0)
    def _():
        for who in [to_east, to_west, across] + others:
            pl.semaphore_signal(barrier, inc=1, device_id=who, device_id_type=MESH)

        lat_pack[...] = jnp.zeros_like(lat_pack)

    unroll = 8

    def group(g, _):
        for sub in range(unroll):
            part = jnp.zeros((8, lanes), F32)
            for slot in range(2):
                at = pl.ds(pl.multiple_of(slot * half + (g * unroll + sub) * 8, 8), 8)
                wet = mask_ref[at, :].astype(F32)
                for k in range(levels):
                    x = state_ref[0, k, at, :] * wet
                    place = 64 * slot + 2 * k
                    part = jnp.where((lane >> 1) == (place >> 1), pltpu.roll(x, place + 1, 1), part)
            to = pl.ds(pl.multiple_of((g * unroll + sub) * 8, 8), 8)
            lat_pack[to, :] += pltpu.roll(part, field * (2 * levels), 1)
        return 0

    lax.fori_loop(0, half // (8 * unroll), group, 0)
    at_field = pl.ds(pl.multiple_of(field * levels, levels), levels)
    first = mask_ref[0:1, :].astype(F32)
    final = mask_ref[rows - 1 : rows, :].astype(F32)
    lon_pack[0, at_field, :] = jnp.concatenate([state_ref[0, k, 0:1, :] for k in range(levels)], 0) * first
    lon_pack[1, at_field, :] = (
        jnp.concatenate([state_ref[0, k, rows - 1 : rows, :] for k in range(levels)], 0) * final
    )

    @pl.when(field == last_field)
    def _():
        chips = devices // 2
        most = jnp.int32(1)
        for chip in range(chips):
            for way in (1, -1):
                number = jnp.int32(0)
                for t in range(4):
                    number = number + leaves(plan_ref, chips, chip, t, way).astype(jnp.int32)
                most = jnp.maximum(most, number)
        count[...] = jnp.full(count.shape, most, jnp.int32)
        pl.semaphore_wait(barrier, 3 + bands - 1)

        def remote(source, target, at, recv_at, who):
            return pltpu.make_async_remote_copy(
                src_ref=source,
                dst_ref=target,
                send_sem=send_sem.at[at],
                recv_sem=recv_sem.at[recv_at],
                device_id=who,
                device_id_type=MESH,
            )

        up = remote(lat_pack, south_in, 0, 0, {"lat": jnp.minimum(lat + 1, bands - 1)})
        down = remote(lat_pack, north_in, 1, 1, {"lat": jnp.maximum(lat - 1, 0)})
        fold = remote(lat_pack, north_in, 0, 1, across)
        east = remote(lon_pack.at[1], west_in, 2, 2, to_east)
        west = remote(lon_pack.at[0], east_in, 3, 3, to_west)
        tell = [remote(count, counts_in.at[o], 4 + o, 4 + o, who) for o, who in enumerate(others)]
        pl.when(top)(fold.start)
        pl.when(jnp.logical_not(top))(up.start)
        pl.when(lat > 0)(down.start)
        east.start()
        west.start()
        for t in tell:
            t.start()

        pl.when(lat > 0)(up.wait_recv)

        @pl.when(lat > 0)
        def _():
            south_ref[...] = south_in[...]

        @pl.when(lat == 0)
        def _():
            south_ref[...] = jnp.zeros_like(south_ref)

        east.wait_recv()
        west_ref[...] = west_in[...]
        west.wait_recv()
        east_ref[...] = east_in[...]
        down.wait_recv()

        @pl.when(top)
        def _():
            r = lax.broadcasted_iota(jnp.int32, (half, half), 0)
            c = lax.broadcasted_iota(jnp.int32, (half, half), 1)
            turn = jnp.where(r + c == half - 1, 1.0, 0.0).astype(F32)
            mirror = jnp.dot(
                turn, north_in[...], precision=lax.Precision.HIGHEST, preferred_element_type=F32
            )
            place = lax.broadcasted_iota(jnp.int32, (half, lanes), 1)
            mirror = pltpu.roll(mirror, 65, 1)
            north_ref[...] = jnp.where((place & 63) >= 32, -mirror, mirror)

        @pl.when(jnp.logical_not(top))
        def _():
            north_ref[...] = north_in[...]

        value = count[...]
        for o, t in enumerate(tell):
            t.wait_recv()
            value = jnp.maximum(value, counts_in[o])
        most_ref[...] = value
        up.wait_send()
        pl.when(lat > 0)(down.wait_send)
        east.wait_send()
        west.wait_send()
        for t in tell:
            t.wait_send()


def halos(plan, state, mask):
    fields, levels, rows, lanes = state.shape
    bands = lax.axis_size("lat")
    pack = (rows // 2, lanes)
    edge = (fields * levels, lanes)
    spec = lambda shape: pl.BlockSpec(shape, lambda f: (0, 0))
    return pl.pallas_call(
        halo_kernel,
        grid=(fields,),
        in_specs=[
            pl.BlockSpec(memory_space=pltpu.SMEM),
            pl.BlockSpec((1, levels, rows, lanes), lambda f: (f, 0, 0, 0)),
            spec((rows, lanes)),
        ],
        out_specs=[spec(pack), spec(pack), spec(edge), spec(edge), spec((8, lanes))],
        out_shape=[
            jax.ShapeDtypeStruct(pack, F32),
            jax.ShapeDtypeStruct(pack, F32),
            jax.ShapeDtypeStruct(edge, F32),
            jax.ShapeDtypeStruct(edge, F32),
            jax.ShapeDtypeStruct((8, lanes), jnp.int32),
        ],
        scratch_shapes=[
            pltpu.VMEM(pack, F32),
            pltpu.VMEM((2,) + edge, F32),
            pltpu.VMEM(pack, F32),
            pltpu.VMEM(pack, F32),
            pltpu.VMEM(edge, F32),
            pltpu.VMEM(edge, F32),
            pltpu.VMEM((8, lanes), jnp.int32),
            pltpu.VMEM((bands - 1, 8, lanes), jnp.int32),
            pltpu.SemaphoreType.DMA((4 + bands - 1,)),
            pltpu.SemaphoreType.DMA((4 + bands - 1,)),
        ],
        compiler_params=pltpu.CompilerParams(
            collective_id=0, has_side_effects=True, vmem_limit_bytes=24 * MIB
        ),
    )(plan, state, mask)


def leaves(plan_ref, chips, chip, t, way):
    target = plan_ref[4 * chip + t] // 4
    return target == lax.rem(chip + way + chips, chips)


def pick(index, values):
    chosen = values[0]
    for at, value in enumerate(values[1:], 1):
        chosen = jnp.where(index == at, value, chosen)
    return chosen


def move_kernel(
    rounds,
    plan_ref,
    state_ref,
    diff_ref,
    mask_ref,
    north_ref,
    south_ref,
    west_ref,
    east_ref,
    out_ref,
    padded,
    mine,
    theirs,
    other,
    other_theirs,
    leaving,
    arrived,
    swapped,
    result,
    load_sem,
    store_sem,
    half_send,
    half_recv,
    tile_send,
    tile_recv,
    swap_send,
    swap_recv,
):
    fields, levels, rows, lanes = state_ref.shape
    quarter = rows // 4
    span = fields // CHUNKS
    devices = lax.axis_size("lon")
    chips = devices // 2
    tiles = 4 * chips
    lon = lax.axis_index("lon")
    chip, core = lon // 2, lax.rem(lon, 2)
    twin = {"lon": lon + 1 - 2 * core}
    ahead = {"lon": lax.rem(lon + 2, devices)}
    behind = {"lon": lax.rem(lon + devices - 2, devices)}
    ways = ((1, ahead), (-1, behind))

    barrier = pltpu.get_barrier_semaphore()
    for who in (twin, ahead, behind):
        pl.semaphore_signal(barrier, inc=1, device_id=who, device_id_type=MESH)

    loads = [
        pltpu.make_async_copy(state_ref.at[f], padded.at[f, :, pl.ds(8, rows), :], load_sem.at[f])
        for f in range(fields)
    ]
    for load in loads:
        load.start()

    chosen = {}
    for side, (way, _) in enumerate(ways):
        hits = [leaves(plan_ref, chips, chip, t, way) for t in range(4)]
        for r in range(rounds):
            count, tile = jnp.int32(0), jnp.int32(0)
            for t in range(4):
                tile = jnp.where(hits[t] & (count == r), t, tile)
                count = count + hits[t].astype(jnp.int32)
            chosen[side, r] = jnp.where(tile // 2 == core, 0, 2) + lax.rem(tile, 2)
    origin = []
    for slot in range(2):
        target = 2 * lon + slot
        source = jnp.int32(0)
        for shift in range(-3, 4):
            g = lax.rem(target + shift + tiles, tiles)
            source = jnp.where(plan_ref[g] == target, g, source)
        from_chip, t = source // 4, lax.rem(source, 4)
        at = jnp.where(t // 2 == core, 0, 2) + lax.rem(t, 2)
        for side, (way, _) in enumerate(ways):
            came = from_chip == lax.rem(chip - way + chips, chips)
            rank = jnp.int32(0)
            for q in range(3):
                hit = leaves(plan_ref, chips, from_chip, q, way) & (q < t)
                rank = rank + hit.astype(jnp.int32)
            at = jnp.where(came, 4 + side * rounds + jnp.minimum(rank, rounds - 1), at)
        origin.append(at)

    for f in range(fields):
        loads[f].wait()

        def cover(g, _):
            for sub in range(2):
                at = pl.ds(pl.multiple_of(g * 16 + sub * 8, 8), 8)
                to = pl.ds(pl.multiple_of(g * 16 + sub * 8 + 8, 8), 8)
                wet = mask_ref[at, :].astype(F32)
                for k in range(levels):
                    padded[f, k, to, :] = padded[f, k, to, :] * wet
            return 0

        lax.fori_loop(0, rows // 16, cover, 0)
        for k in range(levels):
            i = f * levels + k
            padded[f, k, 7:8, :] = west_ref[i : i + 1, :]
            padded[f, k, rows + 8 : rows + 9, :] = east_ref[i : i + 1, :]

    lane = lax.broadcasted_iota(jnp.int32, (8, lanes), 1)
    is_last = lane == lanes - 1
    is_first = lane == 0

    def solve(chunk, half, to_ref):
        work = list(range(chunk * span, chunk * span + span))
        forced = any(f >= 2 for f in work)
        touched = sorted(set(work) | ({0, 1} if forced else set()))

        def group(step, _):
            slot, g = step // (quarter // 8), lax.rem(step, quarter // 8)
            row = pl.multiple_of(half * quarter + g * 8, 8)
            base = pl.multiple_of(slot * (2 * quarter) + row, 8)
            north_pack = pltpu.roll(north_ref[pl.ds(row, 8), :], 64 * slot, 1)
            south_pack = pltpu.roll(south_ref[pl.ds(row, 8), :], 64 * slot, 1)
            wet = mask_ref[pl.ds(base, 8), :].astype(F32)
            zonal = meridional = None
            upper = []
            rhs = []
            for k in range(levels):
                u = padded[2, k, pl.ds(base + 8, 8), :]
                v = padded[3, k, pl.ds(base + 8, 8), :]
                center, grad_x, grad_y, total = {}, {}, {}, {}
                for f in touched:
                    i = f * levels + k
                    center[f] = {2: u, 3: v}.get(f)
                    if f < 2:
                        center[f] = padded[f, k, pl.ds(base + 8, 8), :]
                    e = padded[f, k, pl.ds(base + 9, 8), :]
                    w = padded[f, k, pl.ds(base + 7, 8), :]
                    n = jnp.where(
                        is_last,
                        pltpu.roll(north_pack, (lanes - 1 - (2 * i + 1)) % lanes, 1),
                        pltpu.roll(center[f], lanes - 1, 1),
                    )
                    s = jnp.where(
                        is_first,
                        pltpu.roll(south_pack, (lanes - 2 * i) % lanes, 1),
                        pltpu.roll(center[f], 1, 1),
                    )
                    grad_x[f] = e - w
                    grad_y[f] = n - s
                    if f in work:
                        total[f] = (e + w) + (n + s)
                if forced:
                    dx = haline_coef * grad_x[1] - thermal_coef * grad_x[0]
                    dy = haline_coef * grad_y[1] - thermal_coef * grad_y[0]
                    zonal = dx if k == 0 else zonal + dx
                    meridional = dy if k == 0 else meridional + dy
                lower_k = diff_ref[k - 1, pl.ds(base, 8), :] if k > 0 else None
                upper_k = diff_ref[k, pl.ds(base, 8), :] if k < levels - 1 else None
                pivot = 1.0
                if k > 0:
                    pivot = pivot + lower_k
                if k < levels - 1:
                    pivot = pivot + upper_k
                if k > 0:
                    pivot = pivot - lower_k * upper[k - 1]
                inverse = 1.0 / pivot
                upper.append(upper_k * inverse if k < levels - 1 else None)
                row_rhs = []
                for at, f in enumerate(work):
                    flow = u * grad_x[f] + v * grad_y[f]
                    value = (1.0 - 4.0 * diffuse_coef) * center[f] + (
                        diffuse_coef * total[f] - advect_coef * flow
                    )
                    if f == 2:
                        value = value - (gradient_coef * weight_coef) * zonal
                    if f == 3:
                        value = value - (gradient_coef * weight_coef) * meridional
                    if k > 0:
                        value = value + lower_k * rhs[k - 1][at]
                    row_rhs.append(value * inverse)
                rhs.append(row_rhs)
            to = pl.ds(pl.multiple_of(g * 8, 8), 8)
            for at, f in enumerate(work):
                x = rhs[levels - 1][at]
                to_ref[chunk, slot, at, levels - 1, to, :] = x * wet
                for k in range(levels - 2, -1, -1):
                    x = rhs[k][at] + upper[k] * x
                    to_ref[chunk, slot, at, k, to, :] = x * wet
            return 0

        lax.fori_loop(0, 2 * (quarter // 8), group, 0)

    def remote(source, target, send, recv, who):
        return pltpu.make_async_remote_copy(
            src_ref=source,
            dst_ref=target,
            send_sem=send,
            recv_sem=recv,
            device_id=who,
            device_id_type=MESH,
        )

    pl.semaphore_wait(barrier, 3)
    halves = []
    sent = {}
    for chunk in range(CHUNKS):
        solve(chunk, 1 - core, theirs)
        first = remote(
            theirs.at[chunk], other.at[chunk], half_send.at[chunk, 0], half_recv.at[chunk, 0], twin
        )
        first.start()
        solve(chunk, core, mine)
        second = remote(
            mine.at[chunk], other_theirs.at[chunk], half_send.at[chunk, 1], half_recv.at[chunk, 1], twin
        )
        halves += [first, second]
        first.wait_recv()
        for at in range(span):
            f = chunk * span + at

            def pack(k, _):
                held = [ref[chunk, slot, at, k] for ref in (mine, other) for slot in range(2)]
                for (side, r), index in chosen.items():
                    leaving[f, side, r, k] = pick(index, held)
                return 0

            lax.fori_loop(0, levels, pack, 0)
            for r in range(rounds):
                for side, (_, who) in enumerate(ways):
                    sent[f, side, r] = remote(
                        leaving.at[f, side, r],
                        arrived.at[f, side, r],
                        tile_send.at[f, side, r],
                        tile_recv.at[f, side, r],
                        who,
                    )
                    sent[f, side, r].start()
        second.start()

    keys = [(side, r) for side in range(2) for r in range(rounds)]
    passed = {}
    stores = []
    for chunk in range(CHUNKS):
        halves[2 * chunk + 1].wait_recv()

    def place(f):
        chunk, at = f // span, f % span
        for key in keys:
            passed[(f,) + key].wait_recv()

        def level(k, _):
            for part in range(2):
                held, far, came = (
                    (mine, other, arrived) if part == 0 else (theirs, other_theirs, swapped)
                )
                values = [ref[chunk, slot, at, k] for ref in (held, far) for slot in range(2)]
                values += [came[f, side, r, k] for side, r in keys]
                half = core if part == 0 else 1 - core
                for slot in range(2):
                    row = pl.multiple_of(2 * quarter * slot + half * quarter, quarter)
                    result[f, k, pl.ds(row, quarter), :] = pick(origin[slot], values)
            return 0

        lax.fori_loop(0, levels, level, 0)
        store = pltpu.make_async_copy(result.at[f], out_ref.at[f], store_sem.at[f])
        store.start()
        stores.append(store)

    for f in range(fields):
        for side, r in keys:
            sent[f, side, r].wait_recv()
            passed[f, side, r] = remote(
                arrived.at[f, side, r],
                swapped.at[f, side, r],
                swap_send.at[f, side, r],
                swap_recv.at[f, side, r],
                twin,
            )
            passed[f, side, r].start()
        if f > 0:
            place(f - 1)
    place(fields - 1)
    for copy in halves + list(sent.values()) + list(passed.values()):
        copy.wait_send()
    for store in stores:
        store.wait()


def move(rounds, plan, state, diffusivity, mask, north, south, west, east):
    fields, levels, rows, lanes = state.shape
    quarter = rows // 4
    span = fields // CHUNKS
    anywhere = pl.BlockSpec(memory_space=pl.ANY)
    near = pl.BlockSpec(memory_space=pltpu.VMEM)
    halves = pltpu.VMEM((CHUNKS, 2, span, levels, quarter, lanes), F32)
    pieces = pltpu.VMEM((fields, 2, rounds, levels, quarter, lanes), F32)
    dma = pltpu.SemaphoreType.DMA
    return pl.pallas_call(
        functools.partial(move_kernel, rounds),
        in_specs=[pl.BlockSpec(memory_space=pltpu.SMEM), anywhere] + [near] * 6,
        out_specs=anywhere,
        out_shape=jax.ShapeDtypeStruct(state.shape, F32),
        scratch_shapes=[
            pltpu.VMEM((fields, levels, rows + 16, lanes), F32),
            halves,
            halves,
            halves,
            halves,
            pieces,
            pieces,
            pieces,
            pltpu.VMEM(state.shape, F32),
            dma((fields,)),
            dma((fields,)),
            dma((CHUNKS, 2)),
            dma((CHUNKS, 2)),
            dma((fields, 2, rounds)),
            dma((fields, 2, rounds)),
            dma((fields, 2, rounds)),
            dma((fields, 2, rounds)),
        ],
        compiler_params=pltpu.CompilerParams(
            collective_id=rounds, has_side_effects=True, vmem_limit_bytes=(26 + 6 * rounds) * MIB
        ),
    )(plan, state, diffusivity, mask, north, south, west, east)


def local(state, diffusivity, mask, tile_plan):
    plan = tile_plan.reshape(-1)
    north, south, west, east, most = halos(plan, state, mask)
    branches = [functools.partial(move, rounds) for rounds in (1, 2, 3)]
    which = jnp.clip(most[0, 0] - 1, 0, 2)
    return lax.switch(which, branches, plan, state, diffusivity, mask, north, south, west, east)


def solution(mesh):
    placed = (P(None, None, "lon", "lat"), P(None, "lon", "lat"), P("lon", "lat"), P(None, "lat"))
    return jax.shard_map(
        local, mesh=mesh, in_specs=placed, out_specs=P(None, None, "lon", "lat"), check_vma=False
    )
```

time: 86.2 us -> 73.9 us (0.86)
  Pallas kernels: 22.9 us -> 70.5 us
  waiting for transfers between devices: 42.9 us -> 0 us
  starting transfers between devices: 12.2 us -> 0 us
  local copies, waits for them, and re-layouts: 6.8 us -> 2.54 us
    pallas_call x3 -> x1, Pallas kernels: 12.6 us -> 59.7 us  [move(): pl.pallas_call(functools.partial(move_kernel, rounds), in_specs=[pl.Block...]
    ppermute x10 -> x0, waiting for transfers between devices: 42.9 us -> none  [the longest x4 38.8 us: exchange(): lax.ppermute(send, 'lon', [(i, (i + by) % devices) for i in range(devices)])]
    ppermute x10 -> x0, starting transfers between devices: 12.2 us -> none  [the longest x4 5.48 us: exchange(): swapped = [lax.ppermute(a, 'lon', swap) for a in arrived]]
    unnamed x14 -> x7, local copies, waits for them, and re-layouts: 6.28 us -> 2.03 us
  transfers between devices with their start and end apart: 10 -> 0, of which waited for: 6 -> 0; matrix products, arithmetic and copies ran while one was open for 1% -> 0% of each run, Pallas kernels for 1% -> 0%
where the time goes in v3:
time: 73.9 us; the launch traced here: 73.8 us
  Pallas kernels  70.5 us (95%)
  local copies, waits for them, and re-layouts  2.54 us (3%)
    pallas_call x1, Pallas kernels, move(): pl.pallas_call(functools.partial(move_kernel, rounds), in_specs=[pl.Block...  59.7 us
    pallas_call x1, Pallas kernels, halos(): pl.pallas_call(halo_kernel, grid=(fields,), in_specs=[pl.BlockSpec(memory...  10.8 us
    unnamed x7, local copies, waits for them, and re-layouts  2.03 us

profile of v3, /device:TPU:1, one launch (start us, length us, event | category | flops | bytes accessed | tf_op | source)
XLA Modules:
  0.0 73.8 jit_solution(10603546770592315838)
XLA Ops:
  0.0 0.0 copy-start.1
  0.0 0.0 copy-start
  0.0 0.0 copy-start.2
  0.0 10.8 %shard_map.49 = (f32[128,128]{1,0:T(8,128)S(1)}, f32[128,128]{1,0:T(8,128)S(1)}, f32[32,128]{1,0:T(8,128)S(1)}, f32[32,128]{1,0:T(8,128)S(1)}, s32[8,128]{1,0:T(8,128)S(1)}) custom-call(s32[16]{0:T(128)} %bitcast.2, f32[4,8,256,128]{3,2,1,0:T(8,128)} %state_ref.1, s32[256,128]{1,0:T(8,128)} %mask_ref.1), custom_call_target="tpu_custom_call" | custom-call | tf_op jit(solution)/shard_map/pallas_call | solution.py:177
  10.8 0.5 slice.3
  12.0 0.0 copy-done.1
  12.0 0.0 copy-done
  12.0 0.0 copy-done.2
  12.0 59.7 %conditional.1 = (f32[4,8,256,128]{3,2,1,0:T(8,128)S(1)}) conditional(s32[]{:T(128)} %bitcast.1, (s32[16]{0:T(128)S(1)}, f32[4,8,256,128]{3,2,1,0:T(8,128)S(1)}, f32[7,256,128]{2,1,0:T(8,128)}, s32[256,128]{1,0:T(8,128)S(1)}, f32[128,128]{1,0:T(8,128)S(1)}, /*index=5*/f32[128,128]{1,0:T(8,128)S(1)}, f32[32,128]{1,0:T(8,128)S(1)}, ...), branch_computations={%region_0.1_spmd, %region_1.2_spmd, %region_2.3_spmd} | conditional | bytes 8 | solution.py:546
  12.0 59.7 %branch_0_fun.1 = f32[4,8,256,128]{3,2,1,0:T(8,128)S(1)} custom-call(s32[16]{0:T(128)S(1)} %get-tuple-element.56.plan_ref, f32[4,8,256,128]{3,2,1,0:T(8,128)S(1)} %get-tuple-element.58.state_ref, f32[7,256,128]{2,1,0:T(8,128)} %get-tuple-element.59.diff_ref, s32[256,128]{1,0:T(8,128)S(1)} %get-tuple-element.60.mask_ref, ...), custom_call_target="tpu_custom_call" | custom-call | tf_op jit(solution)/shard_map/cond/branch_0_fun/pallas_call | solution.py:511
  71.7 2.0 %copy.12 = f32[4,8,256,128]{3,2,1,0:T(8,128)} copy(f32[4,8,256,128]{3,2,1,0:T(8,128)S(1)} %get-tuple-element.91) | data formatting | bytes 8388608
Async XLA Ops:
  0.0 12.0 %copy-start.1 = (s32[256,128]{1,0:T(8,128)S(1)}, s32[256,128]{1,0:T(8,128)}, u32[]{:S(2)}) copy-start(s32[256,128]{1,0:T(8,128)} %mask_ref.1) | copy-start | bytes 393220
  0.0 12.0 %copy-start = (f32[4,8,256,128]{3,2,1,0:T(8,128)S(1)}, f32[4,8,256,128]{3,2,1,0:T(8,128)}, u32[]{:S(2)}) copy-start(f32[4,8,256,128]{3,2,1,0:T(8,128)} %state_ref.1) | copy-start | bytes 12582916
  0.0 12.0 %copy-start.2 = (s32[16,1]{0,1:T(1,128)S(1)}, s32[16,1]{0,1:T(1,128)}, u32[]{:S(2)}) copy-start(s32[16,1]{0,1:T(1,128)} %param.10) | copy-start | bytes 196

commit v4 on v3

--- a/solution.py
+++ b/solution.py
@@ -17,7 +17,7 @@
 F32 = jnp.float32
 MIB = 1 << 20
 MESH = pl.DeviceIdType.MESH
-CHUNKS = 2
+CHUNKS = 4
 
 
 def halo_kernel(
@@ -61,7 +61,7 @@
 
         lat_pack[...] = jnp.zeros_like(lat_pack)
 
-    unroll = 8
+    unroll = half // 8
 
     def group(g, _):
         for sub in range(unroll):
@@ -159,7 +159,7 @@
         for o, t in enumerate(tell):
             t.wait_recv()
             value = jnp.maximum(value, counts_in[o])
-        most_ref[...] = value
+        most_ref[0] = jnp.max(value) - 1
         up.wait_send()
         pl.when(lat > 0)(down.wait_send)
         east.wait_send()
@@ -182,13 +182,13 @@
             pl.BlockSpec((1, levels, rows, lanes), lambda f: (f, 0, 0, 0)),
             spec((rows, lanes)),
         ],
-        out_specs=[spec(pack), spec(pack), spec(edge), spec(edge), spec((8, lanes))],
+        out_specs=[spec(pack), spec(pack), spec(edge), spec(edge), pl.BlockSpec(memory_space=pltpu.SMEM)],
         out_shape=[
             jax.ShapeDtypeStruct(pack, F32),
             jax.ShapeDtypeStruct(pack, F32),
             jax.ShapeDtypeStruct(edge, F32),
             jax.ShapeDtypeStruct(edge, F32),
-            jax.ShapeDtypeStruct((8, lanes), jnp.int32),
+            jax.ShapeDtypeStruct((1,), jnp.int32),
         ],
         scratch_shapes=[
             pltpu.VMEM(pack, F32),
@@ -270,8 +270,8 @@
         pltpu.make_async_copy(state_ref.at[f], padded.at[f, :, pl.ds(8, rows), :], load_sem.at[f])
         for f in range(fields)
     ]
-    for load in loads:
-        load.start()
+    for f in (0, 2, 3, 1):
+        loads[f].start()
 
     chosen = {}
     for side, (way, _) in enumerate(ways):
@@ -300,9 +300,7 @@
             at = jnp.where(came, 4 + side * rounds + jnp.minimum(rank, rounds - 1), at)
         origin.append(at)
 
-    for f in range(fields):
-        loads[f].wait()
-
+    def cover_field(f):
         def cover(g, _):
             for sub in range(2):
                 at = pl.ds(pl.multiple_of(g * 16 + sub * 8, 8), 8)
@@ -413,11 +411,16 @@
             device_id_type=MESH,
         )
 
-    pl.semaphore_wait(barrier, 3)
     halves = []
     sent = {}
     for chunk in range(CHUNKS):
+        for f in (0, 2, 3) if chunk == 0 else (1,) if chunk == 1 else ():
+            loads[f].wait()
+        for f in range(chunk * span, chunk * span + span):
+            cover_field(f)
         solve(chunk, 1 - core, theirs)
+        if chunk == 0:
+            pl.semaphore_wait(barrier, 3)
         first = remote(
             theirs.at[chunk], other.at[chunk], half_send.at[chunk, 0], half_recv.at[chunk, 0], twin
         )
@@ -542,8 +545,7 @@
     plan = tile_plan.reshape(-1)
     north, south, west, east, most = halos(plan, state, mask)
     branches = [functools.partial(move, rounds) for rounds in (1, 2, 3)]
-    which = jnp.clip(most[0, 0] - 1, 0, 2)
-    return lax.switch(which, branches, plan, state, diffusivity, mask, north, south, west, east)
+    return lax.switch(most[0], branches, plan, state, diffusivity, mask, north, south, west, east)
 
 
 def solution(mesh):

time: 73.9 us -> 73 us (0.988)
    pallas_call x1, Pallas kernels: 59.7 us -> 57.6 us  [move(): pl.pallas_call(functools.partial(move_kernel, rounds), in_specs=[pl.Block...]
    pallas_call x1, Pallas kernels: 10.8 us -> 12.5 us  [halos(): pl.pallas_call(halo_kernel, grid=(fields,), in_specs=[pl.BlockSpec(memory...]
where the time goes in v4:
time: 73 us; the launch traced here: 72.8 us
  Pallas kernels  70.1 us (96%)
  local copies, waits for them, and re-layouts  2.03 us (3%)
    pallas_call x1, Pallas kernels, move(): pl.pallas_call(functools.partial(move_kernel, rounds), in_specs=[pl.Block...  57.6 us
    pallas_call x1, Pallas kernels, halos(): pl.pallas_call(halo_kernel, grid=(fields,), in_specs=[pl.BlockSpec(memory...  12.5 us
    unnamed x7, local copies, waits for them, and re-layouts  2.03 us

profile of v4, /device:TPU:1, one launch (start us, length us, event | category | flops | bytes accessed | tf_op | source)
XLA Modules:
  0.0 72.8 jit_solution(15628678508104661226)
XLA Ops:
  0.0 0.0 copy-start.1
  0.0 0.0 copy-start
  0.0 0.0 copy-start.2
  0.0 12.5 %shard_map.49 = (f32[128,128]{1,0:T(8,128)S(1)}, f32[128,128]{1,0:T(8,128)S(1)}, f32[32,128]{1,0:T(8,128)S(1)}, f32[32,128]{1,0:T(8,128)S(1)}, s32[1]{0:T(128)}) custom-call(s32[16]{0:T(128)} %bitcast.2, f32[4,8,256,128]{3,2,1,0:T(8,128)} %state_ref.1, s32[256,128]{1,0:T(8,128)} %mask_ref.1), custom_call_target="tpu_custom_call" | custom-call | tf_op jit(solution)/shard_map/pallas_call | solution.py:177
  13.1 0.0 copy-done.1
  13.1 0.0 copy-done
  13.1 0.0 copy-done.2
  13.1 57.7 %conditional.1 = (f32[4,8,256,128]{3,2,1,0:T(8,128)S(1)}) conditional(s32[]{:T(128)} %bitcast.1, (s32[16]{0:T(128)S(1)}, f32[4,8,256,128]{3,2,1,0:T(8,128)S(1)}, f32[7,256,128]{2,1,0:T(8,128)}, s32[256,128]{1,0:T(8,128)S(1)}, f32[128,128]{1,0:T(8,128)S(1)}, /*index=5*/f32[128,128]{1,0:T(8,128)S(1)}, f32[32,128]{1,0:T(8,128)S(1)}, ...), branch_computations={%region_0.0_spmd, %region_1.0_spmd, %region_2.0_spmd} | conditional | bytes 8 | solution.py:548
  13.1 57.6 %branch_0_fun.1 = f32[4,8,256,128]{3,2,1,0:T(8,128)S(1)} custom-call(s32[16]{0:T(128)S(1)} %get-tuple-element.56.plan_ref, f32[4,8,256,128]{3,2,1,0:T(8,128)S(1)} %get-tuple-element.58.state_ref, f32[7,256,128]{2,1,0:T(8,128)} %get-tuple-element.59.diff_ref, s32[256,128]{1,0:T(8,128)S(1)} %get-tuple-element.60.mask_ref, ...), custom_call_target="tpu_custom_call" | custom-call | tf_op jit(solution)/shard_map/cond/branch_0_fun/pallas_call | solution.py:514
  70.8 2.0 %copy.12 = f32[4,8,256,128]{3,2,1,0:T(8,128)} copy(f32[4,8,256,128]{3,2,1,0:T(8,128)S(1)} %get-tuple-element.91) | data formatting | bytes 8388608
Async XLA Ops:
  0.0 13.1 %copy-start.1 = (s32[256,128]{1,0:T(8,128)S(1)}, s32[256,128]{1,0:T(8,128)}, u32[]{:S(2)}) copy-start(s32[256,128]{1,0:T(8,128)} %mask_ref.1) | copy-start | bytes 393220
  0.0 13.1 %copy-start = (f32[4,8,256,128]{3,2,1,0:T(8,128)S(1)}, f32[4,8,256,128]{3,2,1,0:T(8,128)}, u32[]{:S(2)}) copy-start(f32[4,8,256,128]{3,2,1,0:T(8,128)} %state_ref.1) | copy-start | bytes 12582916
  0.0 13.1 %copy-start.2 = (s32[16,1]{0,1:T(1,128)S(1)}, s32[16,1]{0,1:T(1,128)}, u32[]{:S(2)}) copy-start(s32[16,1]{0,1:T(1,128)} %param.10) | copy-start | bytes 196

commit v5 on v4

--- a/solution.py
+++ b/solution.py
@@ -61,7 +61,7 @@
 
         lat_pack[...] = jnp.zeros_like(lat_pack)
 
-    unroll = half // 8
+    unroll = 8
 
     def group(g, _):
         for sub in range(unroll):

time: 73 us -> 72.1 us (0.988)
  Pallas kernels: 70.1 us -> 69.2 us
    pallas_call x1, Pallas kernels: 12.5 us -> 11.6 us  [halos(): pl.pallas_call(halo_kernel, grid=(fields,), in_specs=[pl.BlockSpec(memory...]
where the time goes in v5:
time: 72.1 us; the launch traced here: 71.9 us
  Pallas kernels  69.2 us (96%)
  local copies, waits for them, and re-layouts  2.03 us (3%)
    pallas_call x1, Pallas kernels, move(): pl.pallas_call(functools.partial(move_kernel, rounds), in_specs=[pl.Block...  57.6 us
    pallas_call x1, Pallas kernels, halos(): pl.pallas_call(halo_kernel, grid=(fields,), in_specs=[pl.BlockSpec(memory...  11.6 us
    unnamed x7, local copies, waits for them, and re-layouts  2.03 us

profile of v5, /device:TPU:1, one launch (start us, length us, event | category | flops | bytes accessed | tf_op | source)
XLA Modules:
  0.0 71.9 jit_solution(11233841565918362507)
XLA Ops:
  0.0 0.0 copy-start.1
  0.0 0.0 copy-start
  0.0 0.0 copy-start.2
  0.0 11.6 %shard_map.49 = (f32[128,128]{1,0:T(8,128)S(1)}, f32[128,128]{1,0:T(8,128)S(1)}, f32[32,128]{1,0:T(8,128)S(1)}, f32[32,128]{1,0:T(8,128)S(1)}, s32[1]{0:T(128)}) custom-call(s32[16]{0:T(128)} %bitcast.2, f32[4,8,256,128]{3,2,1,0:T(8,128)} %state_ref.1, s32[256,128]{1,0:T(8,128)} %mask_ref.1), custom_call_target="tpu_custom_call" | custom-call | tf_op jit(solution)/shard_map/pallas_call | solution.py:177
  12.2 0.0 copy-done.1
  12.2 0.0 copy-done
  12.2 0.0 copy-done.2
  12.2 57.7 %conditional.1 = (f32[4,8,256,128]{3,2,1,0:T(8,128)S(1)}) conditional(s32[]{:T(128)} %bitcast.1, (s32[16]{0:T(128)S(1)}, f32[4,8,256,128]{3,2,1,0:T(8,128)S(1)}, f32[7,256,128]{2,1,0:T(8,128)}, s32[256,128]{1,0:T(8,128)S(1)}, f32[128,128]{1,0:T(8,128)S(1)}, /*index=5*/f32[128,128]{1,0:T(8,128)S(1)}, f32[32,128]{1,0:T(8,128)S(1)}, ...), branch_computations={%region_0.0_spmd, %region_1.0_spmd, %region_2.0_spmd} | conditional | bytes 8 | solution.py:548
  12.2 57.6 %branch_0_fun.1 = f32[4,8,256,128]{3,2,1,0:T(8,128)S(1)} custom-call(s32[16]{0:T(128)S(1)} %get-tuple-element.56.plan_ref, f32[4,8,256,128]{3,2,1,0:T(8,128)S(1)} %get-tuple-element.58.state_ref, f32[7,256,128]{2,1,0:T(8,128)} %get-tuple-element.59.diff_ref, s32[256,128]{1,0:T(8,128)S(1)} %get-tuple-element.60.mask_ref, ...), custom_call_target="tpu_custom_call" | custom-call | tf_op jit(solution)/shard_map/cond/branch_0_fun/pallas_call | solution.py:514
  69.9 2.0 %copy.12 = f32[4,8,256,128]{3,2,1,0:T(8,128)} copy(f32[4,8,256,128]{3,2,1,0:T(8,128)S(1)} %get-tuple-element.91) | data formatting | bytes 8388608
Async XLA Ops:
  0.0 12.2 %copy-start.1 = (s32[256,128]{1,0:T(8,128)S(1)}, s32[256,128]{1,0:T(8,128)}, u32[]{:S(2)}) copy-start(s32[256,128]{1,0:T(8,128)} %mask_ref.1) | copy-start | bytes 393220
  0.0 12.2 %copy-start = (f32[4,8,256,128]{3,2,1,0:T(8,128)S(1)}, f32[4,8,256,128]{3,2,1,0:T(8,128)}, u32[]{:S(2)}) copy-start(f32[4,8,256,128]{3,2,1,0:T(8,128)} %state_ref.1) | copy-start | bytes 12582916
  0.0 12.2 %copy-start.2 = (s32[16,1]{0,1:T(1,128)S(1)}, s32[16,1]{0,1:T(1,128)}, u32[]{:S(2)}) copy-start(s32[16,1]{0,1:T(1,128)} %param.10) | copy-start | bytes 196
